TPU v7x, 32 devices: a whole 2x2x4 slice. The times are simulated.
32 devices in a mesh: gx: 4 (over z), gy: 4 (over x, core), role: 2 (over y).
Axes of the slice: x: 2, y: 2, z: 4, core: 2. Of those that a mesh axis runs over, the one named last changes fastest.
Arguments:
- velocity: float32 [3, 64, 64, 256], P(None, 'gx', 'gy', 'role'), may hold values from -6 to 6
- target_visc: bfloat16 [32, 32, 128], P('gx', 'gy', 'role'), may hold values from 0.049804688 to 1
- w_first: bfloat16 [64, 81], replicated, may hold values from -2 to 2
- w_hidden: bfloat16 [64, 1728], replicated, may hold values from -0.3125 to 0.3125
- w_last: bfloat16 [64], replicated, may hold values from -1.5 to 1.5
- sample_owner: int32 [4, 2, 32, 1], P('gy', 'role'), may hold values from 0 to 3; in each aligned block of 8 rows (0 to 7, 8 to 15, ..., all dimensions but the last counted through in order) at most 4 rows name the same one
- sample_block: int32 [4, 2, 32, 1], P('gy', 'role'), may hold values from 0 to 7
Outputs:
- u_next: float32 [3, 64, 64, 256], P(None, 'gx', 'gy', 'role')
- slot_loss: float32 [4, 2, 32], P('gy', 'role', 'gx')
- grad_first: float32 [64, 81], replicated
- grad_hidden: float32 [64, 1728], replicated
- grad_last: float32 [64], replicated
Inputs may be any that keep to these rules, and one draw needn't show every extreme that they name: `sample_owner`: within one trainer's 8 rows (aligned blocks of rows) no gx index is named more than 4 times.
All inputs are finite; a program needn't handle non-finite values.
Results may differ from a plain program's by a relative error of at most 0.002.
The roundings to bfloat16 on the way count: a program that leaves them out, or rounds other values in their place, can miss the bound.
Values may be sent and summed in bfloat16 or wider, within the bound.
No kernel may reach another device: no remote copies, remote signals or barrier semaphores. Data moves between devices by JAX's collectives and lax.ppermute only.
A program may use at most 128 MiB of HBM per device.

v0:
```python
import jax
import jax.numpy as jnp
from jax import lax
from jax.sharding import PartitionSpec as P

BSIDE = 8


base_visc = 0.02
time_step = 0.2


def padded_2(block, sides, width):
    for axis, dim in sides:
        count = lax.axis_size(axis)
        forward = [(i, i + 1) for i in range(count - 1)]
        forward.append((count - 1, 0))
        backward = [(target, source) for source, target in forward]
        low = lax.ppermute(
            lax.slice_in_dim(block, block.shape[dim] - width, None, axis=dim), axis, forward
        )
        high = lax.ppermute(lax.slice_in_dim(block, 0, width, axis=dim), axis, backward)
        block = jnp.concatenate([low, block, high], axis=dim)
    return block


def cell_masks(side):
    count = side**3
    flat = jnp.arange(count, dtype=jnp.int32)
    first = flat // (side * side)
    second = flat // side % side
    third = flat % side
    rows = []
    for k in range(27):
        shift_x = k // 9 - 1
        shift_y = k // 3 % 3 - 1
        shift_z = k % 3 - 1
        inside = (first + shift_x >= 0) & (first + shift_x < side)
        inside = inside & (second + shift_y >= 0) & (second + shift_y < side)
        inside = inside & (third + shift_z >= 0) & (third + shift_z < side)
        rows.append(inside)
    return jnp.stack(rows).astype(jnp.bfloat16)


def pad_cells(field, side):
    reach = side * side + side + 1
    return jnp.pad(field, ((0, 0), (0, 0), (reach, reach)))


def shifted(padded, masks, side, k, count):
    reach = side * side + side + 1
    offset = (k // 9 - 1) * side * side + (k // 3 % 3 - 1) * side + (k % 3 - 1)
    return lax.slice_in_dim(padded, reach + offset, reach + offset + count, axis=2) * masks[k]


def convolve(weight, field, masks, side):
    inner = field.shape[1]
    count = field.shape[2]
    padded = pad_cells(field, side)
    summed = None
    for k in range(27):
        term = jnp.einsum(
            "oc,bcn->bon",
            weight[:, k * inner : (k + 1) * inner],
            shifted(padded, masks, side, k, count),
            preferred_element_type=jnp.float32,
        )
        summed = term if summed is None else summed + term
    return summed


def silu_slope(value):
    sig = jax.nn.sigmoid(value)
    return sig * (1.0 + value * (1.0 - sig))


def network(w_first, w_hidden, w_last, inputs, masks, side):
    pre_first = convolve(w_first, inputs, masks, side)
    act_first = jax.nn.silu(pre_first).astype(jnp.bfloat16)
    pre_hidden = convolve(w_hidden, act_first, masks, side)
    act_hidden = jax.nn.silu(pre_hidden).astype(jnp.bfloat16)
    logits = jnp.einsum("c,bcn->bn", w_last, act_hidden, preferred_element_type=jnp.float32)
    eddy = 0.5 * jax.nn.softplus(logits)
    return (pre_first, act_first, pre_hidden, act_hidden, logits, eddy)


def fit_blocks(w_first, w_hidden, w_last, blocks, masks, side, trainers):
    count = blocks.shape[2]
    width = w_hidden.shape[0]
    inputs = blocks[:, :3]
    target = blocks[:, 3].astype(jnp.float32)
    pre_first, act_first, pre_hidden, act_hidden, logits, eddy = network(
        w_first, w_hidden, w_last, inputs, masks, side
    )
    error = eddy - target
    losses = jnp.mean(error * error, axis=1)
    d_logit = (error * jax.nn.sigmoid(logits) / (trainers * count)).astype(jnp.bfloat16)
    grad_last = jnp.einsum("bn,bcn->c", d_logit, act_hidden, preferred_element_type=jnp.float32)
    d_hidden = (
        w_last.astype(jnp.float32)[None, :, None]
        * d_logit.astype(jnp.float32)[:, None, :]
        * silu_slope(pre_hidden)
    ).astype(jnp.bfloat16)
    padded_act = pad_cells(act_first, side)
    grad_hidden = jnp.concatenate(
        [
            jnp.einsum(
                "bon,bcn->oc",
                d_hidden,
                shifted(padded_act, masks, side, k, count),
                preferred_element_type=jnp.float32,
            )
            for k in range(27)
        ],
        axis=1,
    )
    padded_delta = pad_cells(d_hidden, side)
    d_act = None
    for k in range(27):
        term = jnp.einsum(
            "oc,bon->bcn",
            w_hidden[:, k * width : (k + 1) * width],
            shifted(padded_delta, masks, side, 26 - k, count),
            preferred_element_type=jnp.float32,
        )
        d_act = term if d_act is None else d_act + term
    d_first = (d_act * silu_slope(pre_first)).astype(jnp.bfloat16)
    padded_in = pad_cells(inputs, side)
    grad_first = jnp.concatenate(
        [
            jnp.einsum(
                "bon,bcn->oc",
                d_first,
                shifted(padded_in, masks, side, k, count),
                preferred_element_type=jnp.float32,
            )
            for k in range(27)
        ],
        axis=1,
    )
    return (losses, grad_first, grad_hidden, grad_last)


def to_blocks(field, side):
    chans, size_x, size_y, size_z = field.shape
    split = field.reshape(chans, size_x // side, side, size_y // side, side, size_z // side, side)
    return split.transpose(1, 3, 5, 0, 2, 4, 6).reshape(-1, chans, side**3)


def from_blocks(values, size_x, size_y, size_z, side):
    split = values.reshape(size_x // side, size_y // side, size_z // side, side, side, side)
    return split.transpose(0, 3, 1, 4, 2, 5).reshape(size_x, size_y, size_z)


def window(padded, axis, shift, reach, lead):
    bounds = []
    for dim in range(padded.ndim):
        if dim < lead:
            bounds.append(slice(None))
        else:
            length = padded.shape[dim] - 2 * reach
            opening = reach + (shift if dim == axis else 0)
            bounds.append(slice(opening, opening + length))
    return padded[tuple(bounds)]


def on_device(velocity, target_visc, w_first, w_hidden, w_last, sample_owner, sample_block):
    side = BSIDE
    masks = cell_masks(side)
    comps, cells_x, cells_y, cells_z = velocity.shape
    half_x, half_y, half_z = (cells_x // 2, cells_y // 2, cells_z // 2)
    filtered = (
        velocity.reshape(3, half_x, 2, half_y, 2, half_z, 2)
        .mean(axis=(2, 4, 6))
        .astype(jnp.bfloat16)
    )
    vel_blocks = to_blocks(filtered, side)
    target_blocks = to_blocks(target_visc[None], side)
    stacked = jnp.concatenate([vel_blocks, target_blocks], axis=1)
    eddy = network(w_first, w_hidden, w_last, vel_blocks, masks, side)[5]
    eddy_field = from_blocks(eddy, half_x, half_y, half_z, side)
    eddy_rim = padded_2(eddy_field, (("gx", 0), ("gy", 1), ("role", 2)), 1)
    fine_rim = jnp.repeat(jnp.repeat(jnp.repeat(eddy_rim, 2, 0), 2, 1), 2, 2)
    visc_pad = base_visc + fine_rim[1:-1, 1:-1, 1:-1]
    visc = window(visc_pad, 0, 0, 1, 0)
    vel_pad = padded_2(velocity, (("gx", 1), ("gy", 2), ("role", 3)), 2)
    advect = jnp.zeros_like(velocity)
    diffuse = jnp.zeros_like(velocity)
    for axis in range(3):
        dim = axis + 1
        ahead_one = window(vel_pad, dim, 1, 2, 1)
        behind_one = window(vel_pad, dim, -1, 2, 1)
        ahead_two = window(vel_pad, dim, 2, 2, 1)
        behind_two = window(vel_pad, dim, -2, 2, 1)
        slope = (8.0 * (ahead_one - behind_one) - (ahead_two - behind_two)) / 12.0
        advect = advect + velocity[axis][None] * slope
        visc_ahead = 0.5 * (visc + window(visc_pad, axis, 1, 1, 0))
        visc_behind = 0.5 * (visc + window(visc_pad, axis, -1, 1, 0))
        diffuse = (
            diffuse
            + visc_ahead[None] * (ahead_one - velocity)
            - visc_behind[None] * (velocity - behind_one)
        )
    u_next = velocity + time_step * (diffuse - advect)
    groups = lax.axis_size("gx")
    trainers = groups * lax.axis_size("gy") * lax.axis_size("role")
    slots = sample_owner.shape[2] // groups
    held = stacked.shape[0]
    my_index = lax.axis_index("gx")
    owners = sample_owner.reshape(groups, slots)
    picks = sample_block.reshape(groups, slots)
    my_owners = lax.dynamic_index_in_dim(owners, my_index, 0, keepdims=False)
    my_picks = lax.dynamic_index_in_dim(picks, my_index, 0, keepdims=False)
    wanted = my_owners * held + my_picks
    piece = lax.all_gather(stacked, "gx", axis=0, tiled=True)
    rows = piece.shape[0]
    onehot = (wanted[:, None] == jnp.arange(rows, dtype=jnp.int32)[None, :]).astype(jnp.bfloat16)
    received = jnp.einsum("sr,rcn->scn", onehot, piece, preferred_element_type=jnp.float32).astype(
        jnp.bfloat16
    )
    losses, grad_first, grad_hidden, grad_last = fit_blocks(
        w_first, w_hidden, w_last, received, masks, side, trainers
    )
    grad_first, grad_hidden, grad_last = lax.psum(
        (grad_first, grad_hidden, grad_last), ("gx", "gy", "role")
    )
    slot_loss = losses.reshape(1, 1, slots)
    return (u_next, slot_loss, grad_first, grad_hidden, grad_last)


def solution(mesh):
    return jax.shard_map(
        on_device,
        mesh=mesh,
        in_specs=(
            P(None, "gx", "gy", "role"),
            P("gx", "gy", "role"),
            P(),
            P(),
            P(),
            P("gy", "role", None, None),
            P("gy", "role", None, None),
        ),
        out_specs=(P(None, "gx", "gy", "role"), P("gy", "role", "gx"), P(), P(), P()),
        check_vma=False,
    )
```

profile of v0, /device:TPU:0, one launch (start us, length us, event | category | flops | bytes accessed | tf_op | source)
XLA Modules:
  0.0 281.9 jit_solution(11287658604642485234)
XLA Ops:
  12.6 27.3 %reshape.554 = f32[3,8,2,8,2,64,2]{6,5,4,3,2,1,0:T(8,128)} reshape(f32[3,16,16,128]{3,2,1,0:T(8,128)} %param.7) | data formatting | bytes 786432 | tf_op jit(solution)/shard_map/reshape | solution.py:173
  39.9 9.4 %reduce_sum.18 = f32[3,8,8,64]{3,2,1,0:T(8,128)S(1)} reduce(f32[3,8,2,8,2,64,2]{6,5,4,3,2,1,0:T(8,128)} %reshape.554, f32[]{:T(128)} %constant.188.clone.1), dimensions={2,4,6}, to_apply=%region_0.1 | reduce | flops 86016 | bytes 442372 | tf_op jit(solution)/shard_map/reduce_sum | solution.py:174
  50.6 15.3 %all_gather.3 = bf16[32,4,512]{2,0,1:T(8,128)(2,1)S(1)} all-gather(bf16[8,4,512]{2,0,1:T(8,128)(2,1)S(1)} %pad_maximum_fusion.9), channel_id=1, replica_groups=mesh['gx'=4,'gy'=4,'role'=2] {'gx'}, dimensions={0}, use_global_device_ids=true | all-gather | bytes 163840 | tf_op jit(solution)/shard_map/all_gather | solution.py:215
  122.4 2.0 convolution_bitcast_fusion.11
  134.1 2.0 convolution_bitcast_fusion.10
  142.9 4.8 %fusion.57 = f32[1,8,512]{2,0,1:T(1,128)S(1)} fusion(f32[8,64,512]{2,1,0:T(8,128)} %convolution_bitcast_fusion.10, f32[8,64,512]{2,1,0:T(8,128)} %convolution_bitcast_fusion.11, f32[8,64,512]{2,1,0:T(8,128)} %convolution_bitcast_fusion.12, f32[8,64,512]{2,1,0:T(8,128)} %convolution_bitcast_fusion.13, f32[8,64,512]{2,1,0:T(8,128)} %convolution_bitcast_fusion.14, ...), kind=kOutput, calls=%fused_computation.328 | convolution fusion | flops 39059456 | bytes 11043968 | tf_op jit(solution)/shard_map/c,bcn->bn/dot_general | solution.py:82
  148.2 1.9 collective-permute-start
  150.1 2.0 collective-permute-start.1
  152.8 3.8 %collective-permute-start.6 = (f32[3,2,16,128]{3,2,1,0:T(8,128)}, f32[3,2,16,128]{3,2,1,0:T(8,128)}, u32[]{:S(2)}, u32[]{:S(2)}) collective-permute-start(f32[3,2,16,128]{3,2,1,0:T(8,128)} %get-tuple-element.87), channel_id=1, source_target_pairs={{8,0},{16,8},{24,16},{0,24},{9,1},{17,9},{25,17},{1,25},{10,2},{18... | collective-permute-start | bytes 147464 | tf_op jit(solution)/shard_map/ppermute | solution.py:22
  172.2 1.9 fusion.56
  182.5 1.7 collective-permute-start.3
  187.8 38.9 %all-reduce.5 = (f32[64,81]{0,1:T(8,128)S(1)}, f32[64]{0:T(128)}) all-reduce(f32[64,81]{0,1:T(8,128)S(1)} %concatenate.61, f32[64]{0:T(128)S(1)} %convolution_bitcast_fusion.104), channel_id=1, replica_groups=mesh['gx'=4,'gy'=4,'role'=2] {'gx','gy','role'}, use_global_device_ids=true, to_apply=%region_2.3 | all-reduce | flops 5248 | bytes 41984 | tf_op jit(solution)/shard_map/psum | solution.py:224
  228.6 2.1 reshape.560
  235.0 2.0 collective-permute-start.8
  237.0 3.4 %copy.983 = f32[3,20,16,128]{2,1,3,0:T(8,128)} copy(f32[3,20,16,128]{3,2,1,0:T(8,128)S(1)} %get-tuple-element.95) | data formatting | bytes 983040 | tf_op jit(solution)/shard_map/concatenate | solution.py:23
  240.4 3.3 %copy.982 = f32[3,20,2,128]{2,1,3,0:T(8,128)} copy(f32[3,20,2,128]{3,1,2,0:T(8,128)S(1)} %collective-permute-done.9) | data formatting | bytes 122880 | tf_op jit(solution)/shard_map/ppermute | solution.py:19
  243.8 3.4 %copy.984 = f32[3,20,2,128]{2,1,3,0:T(8,128)} copy(f32[3,20,2,128]{3,1,2,0:T(8,128)S(1)} %collective-permute-done.8) | data formatting | bytes 122880 | tf_op jit(solution)/shard_map/ppermute | solution.py:22
  247.2 7.6 %pad_maximum_fusion = f32[3,20,20,128]{2,1,3,0:T(8,128)S(1)} fusion(f32[3,20,2,128]{2,1,3,0:T(8,128)} %copy.984, f32[3,20,16,128]{2,1,3,0:T(8,128)} %copy.983, f32[3,20,2,128]{2,1,3,0:T(8,128)} %copy.982), kind=kLoop, calls=%fused_computation | loop fusion | flops 307200 | bytes 1228800 | tf_op jit(solution)/shard_map/concatenate | solution.py:23
  254.8 2.1 copy-done.1
  257.6 2.3 collective-permute-start.10
  260.9 3.7 %copy.985 = f32[3,20,20,128]{3,2,1,0:T(8,128)S(1)} copy(f32[3,20,20,128]{2,1,3,0:T(8,128)} %copy-done.1) | data formatting | bytes 1228800 | tf_op jit(solution)/shard_map/concatenate | solution.py:23
  266.7 2.2 copy.987
  269.0 4.0 %fusion.204 = f32[3,16,16,128]{3,2,1,0:T(8,128)} fusion(f32[3,16,16,128]{3,2,1,0:T(8,128)S(1)} %copy-done.3, f32[3,20,20,128]{3,2,1,0:T(8,128)S(1)} %copy.985, f32[3,20,20,2]{3,2,1,0:T(8,128)} %copy.987, f32[3,20,20,2]{3,2,1,0:T(8,128)S(1)} %copy.986, f32[3,20,16,128]{3,2,1,0:T(8,128)} %copy-done.4, f32[3,20,2,128]{3,2,1,0:T(2,128)} %copy.981, ...), kind=kLoop, calls=%fused_computation.428 | loop fusion | flops 4423680 | bytes 4786944 | tf_op jit(solution)/shard_map/add | solution.py:204
  273.0 1.8 copy.1344
  (471 shorter events, 116.1 us)
Async XLA Ops:
  7.2 265.9 %all-reduce.8.cloned.1.call-start = ((), (), s32[]{:S(2)}) async-start(), calls=%async_computation | async-start | bytes 917504 | tf_op jit(solution)/shard_map/psum | solution.py:224
  8.5 130.8 %copy-start.59 = (bf16[512]{0:T(512)(128)(2,1)}, bf16[512]{0:T(512)(128)(2,1)S(1)}, u32[]{:S(2)}) copy-start(bf16[512]{0:T(512)(128)(2,1)S(1)} %get-tuple-element.58) | copy-start | bytes 3076
  8.5 131.2 %copy-start.41 = (bf16[512]{0:T(512)(128)(2,1)}, bf16[512]{0:T(512)(128)(2,1)S(1)}, u32[]{:S(2)}) copy-start(bf16[512]{0:T(512)(128)(2,1)S(1)} %get-tuple-element.57) | copy-start | bytes 3076
  8.5 131.6 %copy-start.43 = (bf16[512]{0:T(512)(128)(2,1)}, bf16[512]{0:T(512)(128)(2,1)S(1)}, u32[]{:S(2)}) copy-start(bf16[512]{0:T(512)(128)(2,1)S(1)} %get-tuple-element.56) | copy-start | bytes 3076
  8.6 132.0 %copy-start.45 = (bf16[512]{0:T(512)(128)(2,1)}, bf16[512]{0:T(512)(128)(2,1)S(1)}, u32[]{:S(2)}) copy-start(bf16[512]{0:T(512)(128)(2,1)S(1)} %get-tuple-element.55) | copy-start | bytes 3076
  8.6 132.4 %copy-start.47 = (bf16[512]{0:T(512)(128)(2,1)}, bf16[512]{0:T(512)(128)(2,1)S(1)}, u32[]{:S(2)}) copy-start(bf16[512]{0:T(512)(128)(2,1)S(1)} %get-tuple-element.54) | copy-start | bytes 3076
  8.6 132.8 %copy-start.49 = (bf16[512]{0:T(512)(128)(2,1)}, bf16[512]{0:T(512)(128)(2,1)S(1)}, u32[]{:S(2)}) copy-start(bf16[512]{0:T(512)(128)(2,1)S(1)} %get-tuple-element.53) | copy-start | bytes 3076
  8.6 133.1 %copy-start.51 = (bf16[512]{0:T(512)(128)(2,1)}, bf16[512]{0:T(512)(128)(2,1)S(1)}, u32[]{:S(2)}) copy-start(bf16[512]{0:T(512)(128)(2,1)S(1)} %get-tuple-element.52) | copy-start | bytes 3076
  8.6 133.5 %copy-start.53 = (bf16[512]{0:T(512)(128)(2,1)}, bf16[512]{0:T(512)(128)(2,1)S(1)}, u32[]{:S(2)}) copy-start(bf16[512]{0:T(512)(128)(2,1)S(1)} %get-tuple-element.51) | copy-start | bytes 3076
  8.6 133.9 %copy-start.55 = (bf16[512]{0:T(512)(128)(2,1)}, bf16[512]{0:T(512)(128)(2,1)S(1)}, u32[]{:S(2)}) copy-start(bf16[512]{0:T(512)(128)(2,1)S(1)} %get-tuple-element.50) | copy-start | bytes 3076
  9.3 129.3 %copy-start.62 = (bf16[512]{0:T(512)(128)(2,1)}, bf16[512]{0:T(512)(128)(2,1)S(1)}, u32[]{:S(2)}) copy-start(bf16[512]{0:T(512)(128)(2,1)S(1)} %get-tuple-element.60) | copy-start | bytes 3076
  9.3 129.7 %copy-start.60 = (bf16[512]{0:T(512)(128)(2,1)}, bf16[512]{0:T(512)(128)(2,1)S(1)}, u32[]{:S(2)}) copy-start(bf16[512]{0:T(512)(128)(2,1)S(1)} %get-tuple-element.59) | copy-start | bytes 3076
  148.2 34.2 %collective-permute-start = (f32[1,8,64]{2,1,0:T(8,128)S(1)}, f32[1,8,64]{2,1,0:T(8,128)S(1)}, u32[]{:S(2)}, u32[]{:S(2)}) collective-permute-start(f32[1,8,64]{2,1,0:T(8,128)S(1)} %slice.1198), channel_id=1, source_target_pairs={{0,8},{8,16},{16,24},{24,0},{1,9},{9,17},{17,25},{25,1},{2,10},{10... | collective-permute-start | bytes 6152 | tf_op jit(solution)/shard_map/ppermute | solution.py:19
  150.1 32.3 %collective-permute-start.1 = (f32[1,8,64]{2,1,0:T(8,128)S(1)}, f32[1,8,64]{2,1,0:T(8,128)S(1)}, u32[]{:S(2)}, u32[]{:S(2)}) collective-permute-start(f32[1,8,64]{2,1,0:T(8,128)S(1)} %slice.1200), channel_id=1, source_target_pairs={{8,0},{16,8},{24,16},{0,24},{9,1},{17,9},{25,17},{1,25},{10,2},{18... | collective-permute-start | bytes 6152 | tf_op jit(solution)/shard_map/ppermute | solution.py:22
  152.7 80.3 %collective-permute-start.7 = (f32[3,2,16,128]{3,2,1,0:T(8,128)}, f32[3,2,16,128]{3,2,1,0:T(8,128)}, u32[]{:S(2)}, u32[]{:S(2)}) collective-permute-start(f32[3,2,16,128]{3,2,1,0:T(8,128)} %get-tuple-element.88), channel_id=1, source_target_pairs={{0,8},{8,16},{16,24},{24,0},{1,9},{9,17},{17,25},{25,1},{2,10},{10... | collective-permute-start | bytes 147464 | tf_op jit(solution)/shard_map/ppermute | solution.py:19
  152.8 81.2 %collective-permute-start.6 = (f32[3,2,16,128]{3,2,1,0:T(8,128)}, f32[3,2,16,128]{3,2,1,0:T(8,128)}, u32[]{:S(2)}, u32[]{:S(2)}) collective-permute-start(f32[3,2,16,128]{3,2,1,0:T(8,128)} %get-tuple-element.87), channel_id=1, source_target_pairs={{8,0},{16,8},{24,16},{0,24},{9,1},{17,9},{25,17},{1,25},{10,2},{18... | collective-permute-start | bytes 147464 | tf_op jit(solution)/shard_map/ppermute | solution.py:22
  182.5 3.1 %collective-permute-start.2 = (f32[10,1,64]{2,1,0:T(1,128)S(1)}, f32[10,1,64]{2,1,0:T(1,128)S(1)}, u32[]{:S(2)}, u32[]{:S(2)}) collective-permute-start(f32[10,1,64]{2,1,0:T(1,128)S(1)} %get-tuple-element.98), channel_id=1, source_target_pairs={{0,2},{2,4},{4,6},{6,0},{1,3},{3,5},{5,7},{7,1},{8,10},{10,12},{12... | collective-permute-start | bytes 7688 | tf_op jit(solution)/shard_map/ppermute | solution.py:19
  182.5 3.1 %collective-permute-start.3 = (f32[10,1,64]{2,1,0:T(1,128)S(1)}, f32[10,1,64]{2,1,0:T(1,128)S(1)}, u32[]{:S(2)}, u32[]{:S(2)}) collective-permute-start(f32[10,1,64]{2,1,0:T(1,128)S(1)} %get-tuple-element.99), channel_id=1, source_target_pairs={{2,0},{4,2},{6,4},{0,6},{3,1},{5,3},{7,5},{1,7},{10,8},{12,10},{14... | collective-permute-start | bytes 7688 | tf_op jit(solution)/shard_map/ppermute | solution.py:22
  185.7 41.7 %collective-permute-start.4 = (f32[10,10,1]{2,1,0:T(8,128)S(1)}, f32[10,10,1]{2,1,0:T(8,128)S(1)}, u32[]{:S(2)}, u32[]{:S(2)}) collective-permute-start(f32[10,10,1]{2,1,0:T(8,128)S(1)} %get-tuple-element.91), channel_id=1, source_target_pairs={{0,1},{1,0},{2,3},{3,2},{4,5},{5,4},{6,7},{7,6},{8,9},{9,8},{10,11... | collective-permute-start | bytes 1208 | tf_op jit(solution)/shard_map/ppermute | solution.py:19
  187.3 40.1 %collective-permute-start.5 = (f32[10,10,1]{2,1,0:T(8,128)S(1)}, f32[10,10,1]{2,1,0:T(8,128)S(1)}, u32[]{:S(2)}, u32[]{:S(2)}) collective-permute-start(f32[10,10,1]{2,1,0:T(8,128)S(1)} %get-tuple-element.92), channel_id=1, source_target_pairs={{1,0},{0,1},{3,2},{2,3},{5,4},{4,5},{7,6},{6,7},{9,8},{8,9},{11,10... | collective-permute-start | bytes 1208 | tf_op jit(solution)/shard_map/ppermute | solution.py:22
  234.9 5.5 %collective-permute-start.9 = (f32[3,20,2,128]{3,1,2,0:T(8,128)S(1)}, f32[3,20,2,128]{3,1,2,0:T(8,128)S(1)}, u32[]{:S(2)}, u32[]{:S(2)}) collective-permute-start(f32[3,20,2,128]{3,1,2,0:T(8,128)S(1)} %copy.1158), channel_id=1, source_target_pairs={{0,2},{2,4},{4,6},{6,0},{1,3},{3,5},{5,7},{7,1},{8,10},{10,12},{12... | collective-permute-start | bytes 184328 | tf_op jit(solution)/shard_map/ppermute | solution.py:19
  235.0 8.8 %collective-permute-start.8 = (f32[3,20,2,128]{3,1,2,0:T(8,128)S(1)}, f32[3,20,2,128]{3,1,2,0:T(8,128)S(1)}, u32[]{:S(2)}, u32[]{:S(2)}) collective-permute-start(f32[3,20,2,128]{3,1,2,0:T(8,128)S(1)} %copy.1157), channel_id=1, source_target_pairs={{2,0},{4,2},{6,4},{0,6},{3,1},{5,3},{7,5},{1,7},{10,8},{12,10},{14... | collective-permute-start | bytes 184328 | tf_op jit(solution)/shard_map/ppermute | solution.py:22
  257.6 7.8 %collective-permute-start.10 = (f32[3,20,20,2]{2,1,3,0:T(8,128)S(1)}, f32[3,20,20,2]{2,1,3,0:T(8,128)}, u32[]{:S(2)}, u32[]{:S(2)}) collective-permute-start(f32[3,20,20,2]{2,1,3,0:T(8,128)S(1)} %get-tuple-element.71), channel_id=1, source_target_pairs={{1,0},{0,1},{3,2},{2,3},{5,4},{4,5},{7,6},{6,7},{9,8},{8,9},{11,10... | collective-permute-start | bytes 28808 | tf_op jit(solution)/shard_map/ppermute | solution.py:22
  259.8 6.9 %collective-permute-start.11 = (f32[3,20,20,2]{2,1,3,0:T(8,128)}, f32[3,20,20,2]{2,1,3,0:T(8,128)}, u32[]{:S(2)}, u32[]{:S(2)}) collective-permute-start(f32[3,20,20,2]{2,1,3,0:T(8,128)} %get-tuple-element.72), channel_id=1, source_target_pairs={{0,1},{1,0},{2,3},{3,2},{4,5},{5,4},{6,7},{7,6},{8,9},{9,8},{10,11... | collective-permute-start | bytes 28808 | tf_op jit(solution)/shard_map/ppermute | solution.py:19
  (80 other events, 1879.6 us)
Sparse Core Ops, SparseCore 0:
  108.8 127.6 all-reduce.7
where the time goes:
time: 286 us; the launch traced here: 282 us
  matrix products  96.7 us (34%)
  local copies, waits for them, and re-layouts  64.8 us (23%)
  blocking collectives  54.2 us (19%)
  other arithmetic  33.1 us (12%)
  between operations  16.9 us (6%)
  starting transfers between devices  15.9 us (6%)
    dot_general x107, matrix products, convolve(): jnp.einsum('oc,bcn->bon', weight[:, k * inner:(k + 1) * inner], shifted(p...  55.4 us
    psum x1, blocking collectives, on_device(): lax.psum((grad_first, grad_hidden, grad_last), ('gx', 'gy', 'role'))  38.9 us
    reshape x1, local copies, waits for them, and re-layouts, on_device(): velocity.reshape(3, half_x, 2, half_y, 2, half_z, 2).mean(axis=(2, 4, 6))  27.3 us
    dot_general x27, matrix products, fit_blocks(): jnp.einsum('oc,bon->bcn', w_hidden[:, k * width:(k + 1) * width], shifted...  16.9 us
    all_gather x1, blocking collectives, on_device(): piece = lax.all_gather(stacked, 'gx', axis=0, tiled=True)  15.3 us
    dot_general x27, matrix products, fit_blocks(): jnp.einsum('bon,bcn->oc', d_hidden, shifted(padded_act, masks, side, k, c...  12.3 us
    ppermute x6, starting transfers between devices, padded_2(): lax.ppermute(lax.slice_in_dim(block, 0, width, axis=dim), axis, backward)  12.2 us
    reduce_sum x1, other arithmetic, on_device(): filtered = velocity.reshape(3, half_x, 2, half_y, 2, half_z, 2).mean(axis...  9.44 us
  transfers between devices with their start and end apart: 13, of which 1 were waited for; matrix products, arithmetic and copies ran while one was open for 37% of the time, Pallas kernels for 0%

commit v1 on v0

v1 whole, which is shorter than its diff:
```python
import jax
import jax.numpy as jnp
from jax import lax
from jax.experimental import pallas as pl
from jax.experimental.pallas import tpu as pltpu
from jax.sharding import PartitionSpec as P

F32 = jnp.float32
BF16 = jnp.bfloat16
HIGH = lax.Precision.HIGHEST

SIDE = 8
CELLS = SIDE**3
CH = 64
BLK = 8
ROWS = SIDE * SIDE * BLK
WIDE = SIDE * CH
SLAB = SIDE * BLK
GRAD_AT = 128
PAY = 1920
LAST_COL = 81
LOSS_COL = 82

base_visc = 0.02
time_step = 0.2


def iota(shape, dim):
    return lax.broadcasted_iota(jnp.int32, shape, dim)


def onehot(cond, dtype=BF16):
    return jnp.where(cond, 1.0, 0.0).astype(dtype)


def nt(a, b, precision=None):
    return lax.dot_general(a, b, (((1,), (1,)), ((), ())), preferred_element_type=F32, precision=precision)


def tn(a, b, precision=None):
    return lax.dot_general(a, b, (((0,), (0,)), ((), ())), preferred_element_type=F32, precision=precision)


def nn(a, b, precision=None):
    return lax.dot_general(a, b, (((1,), (0,)), ((), ())), preferred_element_type=F32, precision=precision)


def net_kernel(
    scal, vel, tgt, w1, w2, w3, own, blk,
    keep, send, eddy_out, hx_a, hx_b, hy_a, hy_b, hz,
    pool_s, fp_s, i1_s, a_s, d_s, tt_s, tb_s, pre_s, slope1_s, ah_s, slope2_s, dw_s, big_s, gh_s,
):
    trainers = scal[0, 0]
    gx_at = scal[0, 1]
    gy_at = scal[0, 2]
    half = scal[0, 3]
    dev = scal[0, 4]
    gx_odd = gx_at % 2 == 1
    gy_odd = gy_at % 2 == 1

    for c in range(3):
        for x in range(SIDE):
            both = vel[c, 2 * x] + vel[c, 2 * x + 1]
            pool_s[c, x] = both
    rows = []
    for c in range(3):
        cols = []
        for x in range(SIDE):
            cols.append(pool_s[c, x, pl.ds(0, 8, stride=2), :] + pool_s[c, x, pl.ds(1, 8, stride=2), :])
        rows.append(jnp.concatenate(cols, axis=0))
    pooled = jnp.concatenate(rows, axis=0)
    zpool = jnp.where(iota((128, 64), 0) // 2 == iota((128, 64), 1), 0.125, 0.0).astype(F32)
    filt = nn(pooled, zpool, HIGH).astype(BF16)
    tgt_rows = tgt[...].reshape(64, 64)
    zsel = jnp.concatenate([filt[0:64], filt[64:128], filt[128:192], tgt_rows], axis=1)
    spread = onehot(iota((ROWS, 64), 0) // BLK == iota((ROWS, 64), 1))
    by_block = nn(spread, zsel)
    mine = (iota((ROWS, 256), 1) % 64) // SIDE == iota((ROWS, 256), 0) % BLK
    by_block = jnp.where(mine, by_block, 0.0).astype(BF16)
    src_c = iota((256, 256), 0) // 64
    src_z = iota((256, 256), 0) % SIDE
    dst = iota((256, 256), 1)
    pick = onehot((dst < 216) & ((dst % 24) // SIDE == src_c) & (dst % SIDE == src_z))
    cells = nn(by_block, pick)
    dst8 = iota((256, SIDE), 1)
    pick_t = onehot((iota((256, SIDE), 0) // 64 == 3) & (iota((256, SIDE), 0) % SIDE == dst8))
    target = nn(by_block, pick_t)

    fp_s[...] = jnp.zeros(fp_s.shape, F32)
    fp_s[1:9, 1:9] = cells.reshape(SIDE, SIDE, BLK, 256)
    group = iota((1, 1, 1, 256), 3) // 24
    for x in range(SIDE):
        acc = jnp.zeros((1, SIDE, BLK, 256), F32)
        for k in range(9):
            part = fp_s[x + k // 3 : x + k // 3 + 1, k % 3 : k % 3 + SIDE]
            acc = jnp.where(group == k, part, acc)
        i1_s[x * SLAB : (x + 1) * SLAB, :] = acc.reshape(SLAB, 256).astype(BF16)

    j_at = iota((81, 256), 0)
    l_at = iota((81, 256), 1)
    same = (l_at < 216) & (j_at // 9 == l_at // 24) & (j_at % 3 == (l_at % 24) // SIDE)
    delta = l_at % SIDE - ((j_at // 3) % 3 - 1)
    w1v = w1[...]
    t1 = jnp.concatenate([nn(w1v, onehot(same & (delta == z))).astype(BF16) for z in range(SIDE)], axis=0)
    pre_s[...] = nt(i1_s[...], t1)

    src = iota((256, 512), 0)
    dst = iota((256, 512), 1)
    d_of = dst // 128 - 2
    half_of = (dst % 128) // 64
    zero_tile = jnp.zeros((64, 128), BF16)
    for k in range(9):
        base = (192 * k) // 128 * 128
        off = 192 * k - base
        width = min(256, 1728 - base)
        rel = src - off
        chooser = onehot((rel >= 0) & (rel < 192) & (rel // 64 - 1 == d_of + half_of) & (rel % 64 == dst % 64))
        tiles = nn(w2[:, base : base + width], chooser[:width]).astype(BF16)
        ks, js = k // 3, k % 3
        kb, jb = (8 - k) // 3, (8 - k) % 3
        for z in range(SIDE):
            for m in range(4):
                d = 2 * m - z
                tile = tiles[:, (d + 2) * 128 : (d + 3) * 128] if -2 <= d <= 1 else zero_tile
                tt_s[ks, z * 64 : (z + 1) * 64, js * 512 + m * 128 : js * 512 + (m + 1) * 128] = tile
                tb_s[kb, jb * 512 + z * 64 : jb * 512 + (z + 1) * 64, m * 128 : (m + 1) * 128] = tile

    def shifted_store(dst_ref, x, val):
        zero = jnp.zeros((1, BLK, WIDE), F32)
        lo, hi = (x + 1) * SLAB, (x + 2) * SLAB
        dst_ref[lo:hi, 0:512] = jnp.concatenate([zero, val[:-1]], axis=0).reshape(SLAB, WIDE).astype(BF16)
        dst_ref[lo:hi, 512:1024] = val.reshape(SLAB, WIDE).astype(BF16)
        dst_ref[lo:hi, 1024:1536] = jnp.concatenate([val[1:], zero], axis=0).reshape(SLAB, WIDE).astype(BF16)

    for ref in (a_s, d_s):
        ref[0:SLAB, :] = jnp.zeros((SLAB, 1536), BF16)
        ref[9 * SLAB :, :] = jnp.zeros((SLAB, 1536), BF16)

    for x in range(SIDE):
        pre = pre_s[x * SLAB : (x + 1) * SLAB, :]
        sig = jax.nn.sigmoid(pre)
        slope1_s[x * SLAB : (x + 1) * SLAB, :] = sig * (1.0 + pre * (1.0 - sig))
        shifted_store(a_s, x, (pre * sig).reshape(SIDE, BLK, WIDE))

    acc = nt(a_s[0:ROWS, :], tt_s[0])
    acc = acc + nt(a_s[SLAB : SLAB + ROWS, :], tt_s[1])
    pre_s[...] = acc + nt(a_s[2 * SLAB : 2 * SLAB + ROWS, :], tt_s[2])
    for x in range(SIDE):
        pre = pre_s[x * SLAB : (x + 1) * SLAB, :]
        sig = jax.nn.sigmoid(pre)
        slope2_s[x * SLAB : (x + 1) * SLAB, :] = sig * (1.0 + pre * (1.0 - sig))
        ah_s[x * SLAB : (x + 1) * SLAB, :] = (pre * sig).astype(BF16)

    tile8 = onehot(iota((64, WIDE), 0) == iota((64, WIDE), 1) % 64)
    w3_wide = nn(w3[...], tile8)
    last = jnp.where(iota((SIDE, WIDE), 1) // 64 == iota((SIDE, WIDE), 0), w3_wide, 0.0).astype(BF16)
    logits = nt(ah_s[...], last)
    eddy = 0.5 * (jnp.maximum(logits, 0.0) + jnp.log1p(jnp.exp(-jnp.abs(logits))))
    error = eddy - target
    losses = jnp.sum(jnp.sum((error * error).reshape(64, BLK, SIDE), axis=0), axis=1, keepdims=True) / CELLS
    d_logit = (error * jax.nn.sigmoid(logits) / (trainers.astype(F32) * CELLS)).astype(BF16)

    zrep = onehot(iota((SIDE, 128), 0) == (iota((SIDE, 128), 1) % 16) // 2, F32)
    fine = nn(eddy, zrep, HIGH)
    fine = jnp.where(iota((ROWS, 128), 1) // 16 == iota((ROWS, 128), 0) % BLK, fine, 0.0)
    fine = jnp.sum(fine.reshape(64, BLK, 128), axis=1)
    eddy_out[...] = fine

    for c in range(3):
        for i in range(2):
            lo, hi = vel[c, i], vel[c, 14 + i]
            at = (c * 2 + i) * 16
            hx_a[at : at + 16, :] = jnp.where(gx_odd, lo, hi)
            hx_b[at : at + 16, :] = jnp.where(gx_odd, hi, lo)
    hx_a[96:104, :] = jnp.where(gx_odd, fine[0:8], fine[56:64])
    hx_b[96:104, :] = jnp.where(gx_odd, fine[56:64], fine[0:8])
    for c in range(3):
        for i in range(2):
            lo = jnp.concatenate([vel[c, x, i : i + 1, :] for x in range(16)], axis=0)
            hi = jnp.concatenate([vel[c, x, 14 + i : 15 + i, :] for x in range(16)], axis=0)
            at = (c * 2 + i) * 16
            hy_a[at : at + 16, :] = jnp.where(gy_odd, lo, hi)
            hy_b[at : at + 16, :] = jnp.where(gy_odd, hi, lo)
    lo = eddy_out[pl.ds(0, 8, stride=8), :]
    hi = eddy_out[pl.ds(7, 8, stride=8), :]
    hy_a[96:104, :] = jnp.where(gy_odd, lo, hi)
    hy_b[96:104, :] = jnp.where(gy_odd, hi, lo)
    vt = jnp.transpose(vel[...].reshape(768, 128))
    hz[...] = jnp.zeros(hz.shape, F32)
    hz[0:2, 0:768] = vt[0:2]
    hz[2:4, 0:768] = vt[126:128]
    et = jnp.transpose(jnp.concatenate([fine, jnp.zeros((64, 128), F32)], axis=0))
    hz[0:1, 768:896] = et[0:1]
    hz[1:2, 768:896] = et[127:128]

    code = own[...] * BLK + blk[...]
    listed = code.shape[1]
    wanted = gx_at * BLK + iota((BLK, listed), 0)
    count = jnp.sum(jnp.where(code == wanted, 1.0, 0.0), axis=1, keepdims=True)
    count_rows = jnp.broadcast_to(count.reshape(1, BLK, 1), (64, BLK, 1)).reshape(ROWS, 1)

    big_s[:, 0:512] = nn(d_logit, last)
    for x in range(SIDE):
        d_hid = big_s[x * SLAB : (x + 1) * SLAB, 0:512] * slope2_s[x * SLAB : (x + 1) * SLAB, :]
        d_hid = d_hid.astype(BF16).astype(F32).reshape(SIDE, BLK, WIDE)
        shifted_store(d_s, x, d_hid)
        dw_s[x * SLAB : (x + 1) * SLAB, :] = (d_hid * count[None]).reshape(SLAB, WIDE)
    dwt = jnp.transpose(dw_s[...]).astype(BF16)

    gh_s[...] = jnp.zeros(gh_s.shape, F32)
    low_half = iota((64, 128), 1) < 64
    for k in range(9):
        dx, j = k // 3, k % 3
        big_s[:, 0:512] = nn(dwt, a_s[dx * SLAB : dx * SLAB + ROWS, j * 512 : (j + 1) * 512])
        sums = []
        for m in (-1, 0, 1, 2):
            tot = None
            for p in range(4):
                z = 2 * p + m
                if 0 <= z < SIDE:
                    part = big_s[z * 64 : (z + 1) * 64, p * 128 : (p + 1) * 128]
                    tot = part if tot is None else tot + part
            sums.append(tot)
        for dz in (-1, 0, 1):
            low, high = sums[1 - dz], sums[2 - dz]
            at = (k * 3 + dz + 1) * 64
            tile, odd = at // 128 * 128, at % 128 != 0
            if odd:
                val = high + pltpu.roll(low, 64, 1)
                gh_s[:, tile : tile + 128] += jnp.where(low_half, 0.0, val)
            else:
                val = low + pltpu.roll(high, 64, 1)
                gh_s[:, tile : tile + 128] += jnp.where(low_half, val, 0.0)

    acc = nn(d_s[0:ROWS, :], tb_s[0])
    acc = acc + nn(d_s[SLAB : SLAB + ROWS, :], tb_s[1])
    acc = acc + nn(d_s[2 * SLAB : 2 * SLAB + ROWS, :], tb_s[2])
    d_first = (acc * slope1_s[...]).astype(BF16).astype(F32)
    dw_s[...] = (d_first.reshape(64, BLK, WIDE) * count[None]).reshape(ROWS, WIDE)
    d1t = jnp.transpose(dw_s[...])
    d1_hi = d1t.astype(BF16)
    d1_lo = (d1t - d1_hi.astype(F32)).astype(BF16)
    i1 = i1_s[...]
    g1 = nn(d1_hi, i1) + nn(d1_lo, i1)
    z_in = iota((64, 256), 1) % SIDE
    parts = []
    for dz in (-1, 0, 1):
        tot = jnp.zeros((64, 256), F32)
        for z in range(SIDE):
            if 0 <= z + dz < SIDE:
                tot = tot + jnp.where(z_in == z + dz, g1[z * 64 : (z + 1) * 64], 0.0)
        parts.append(tot)
    r_at = iota((768, 128), 0)
    c_at = iota((768, 128), 1)
    l_at = r_at % 256
    fold = onehot(
        (l_at < 216) & (c_at // 9 == l_at // 24) & ((c_at // 3) % 3 == r_at // 256) & (c_at % 3 == (l_at % 24) // SIDE)
        & (c_at < 81),
        F32,
    )
    g_first = nn(jnp.concatenate(parts, axis=1), fold, HIGH)

    dlw = d_logit.astype(F32) * count_rows
    dl_hi = dlw.astype(BF16)
    dl_lo = (dlw - dl_hi.astype(F32)).astype(BF16)
    ah = ah_s[...]
    gl = tn(dl_hi, ah) + tn(dl_lo, ah)
    gl = jnp.where(iota((SIDE, WIDE), 1) // 64 == iota((SIDE, WIDE), 0), gl, 0.0)
    fold_o = onehot(iota((64, WIDE), 1) % 64 == iota((64, WIDE), 0), F32)
    g_last = jnp.sum(nt(fold_o, gl, HIGH), axis=1, keepdims=True)

    lane8 = iota((BLK, 128), 1)
    loss_row = jnp.where(lane8 - (LOSS_COL + BLK * (dev // 64)) == iota((BLK, 128), 0), losses, 0.0)
    loss_row = jnp.sum(loss_row, axis=0, keepdims=True)
    lane = iota((64, 128), 1)
    extra = jnp.where(lane == LAST_COL, g_last, g_first)
    extra = extra + jnp.where(iota((64, 128), 0) == dev % 64, loss_row, 0.0)

    second = half == 1
    keep[:, 0:128] = jnp.where(second, extra[32:64], extra[0:32])
    send[:, 0:128] = jnp.where(second, extra[0:32], extra[32:64])
    top, bottom = gh_s[0:32, :], gh_s[32:64, :]
    keep[:, 128:PAY] = jnp.where(second, bottom, top)
    send[:, 128:PAY] = jnp.where(second, top, bottom)


def vmem_spec():
    return pl.BlockSpec(memory_space=pltpu.VMEM)


def run_net(scal, velocity, target, w1, w2, w3, own, blk):
    f = lambda *s: jax.ShapeDtypeStruct(s, F32)
    return pl.pallas_call(
        net_kernel,
        out_shape=(f(32, PAY), f(32, PAY), f(64, 128), f(104, 128), f(104, 128), f(104, 128), f(104, 128), f(8, 896)),
        in_specs=[pl.BlockSpec(memory_space=pltpu.SMEM)] + [vmem_spec()] * 7,
        out_specs=tuple(vmem_spec() for _ in range(8)),
        scratch_shapes=[
            pltpu.VMEM((3, SIDE, 16, 128), F32),
            pltpu.VMEM((10, 10, BLK, 256), F32),
            pltpu.VMEM((ROWS, 256), BF16),
            pltpu.VMEM((ROWS + 2 * SLAB, 1536), BF16),
            pltpu.VMEM((ROWS + 2 * SLAB, 1536), BF16),
            pltpu.VMEM((3, 512, 1536), BF16),
            pltpu.VMEM((3, 1536, 512), BF16),
            pltpu.VMEM((ROWS, WIDE), F32),
            pltpu.VMEM((ROWS, WIDE), F32),
            pltpu.VMEM((ROWS, WIDE), BF16),
            pltpu.VMEM((ROWS, WIDE), F32),
            pltpu.VMEM((ROWS, WIDE), F32),
            pltpu.VMEM((ROWS, WIDE), F32),
            pltpu.VMEM((64, PAY - 128), F32),
        ],
        compiler_params=pltpu.CompilerParams(vmem_limit_bytes=56 * 1024 * 1024),
        name="net",
    )(scal, velocity, target, w1, w2, w3, own, blk)


def flow_kernel(scal, vel, eddy, rx_a, rx_b, ry_a, ry_b, rz, out, vx_s, vy_s, visc_s, ez_s, fine_s):
    gx_odd = scal[0, 1] % 2 == 1
    gy_odd = scal[0, 2] % 2 == 1
    lane = iota((1, 128), 1)

    def sides(odd, a, b, at, rows):
        one, two = a[at : at + rows, :], b[at : at + rows, :]
        return jnp.where(odd, one, two), jnp.where(odd, two, one)

    for c in range(3):
        for x in range(16):
            vy_s[(c * 16 + x) * 32 + 8 : (c * 16 + x) * 32 + 24, :] = vel[c, x]
        for i in range(2):
            below, above = sides(gy_odd, ry_a, ry_b, (c * 2 + i) * 16, 16)
            vy_s[pl.ds(c * 512 + 6 + i, 16, stride=32), :] = below
            vy_s[pl.ds(c * 512 + 24 + i, 16, stride=32), :] = above
            below, above = sides(gx_odd, rx_a, rx_b, (c * 2 + i) * 16, 16)
            vx_s[c, i] = below
            vx_s[c, 2 + i] = above

    zcols = jnp.transpose(rz[...])
    coarse = eddy[...]
    e_first, e_last = zcols[768:832, 0:1], zcols[768:832, 1:2]
    ahead = jnp.where(lane == 127, e_first, pltpu.roll(coarse, 127, 1))
    behind = jnp.where(lane == 0, e_last, pltpu.roll(coarse, 1, 1))
    below_x, above_x = sides(gx_odd, rx_a, rx_b, 96, 8)
    below_y, above_y = sides(gy_odd, ry_a, ry_b, 96, 8)

    def put(dst, plane, val):
        dst[pl.ds(plane * 32 + 8, 8, stride=2), :] = val
        dst[pl.ds(plane * 32 + 9, 8, stride=2), :] = val

    put(visc_s, 0, base_visc + below_x)
    put(visc_s, 17, base_visc + above_x)
    for x in range(8):
        for r in range(2):
            plane = 2 * x + 1 + r
            put(visc_s, plane, base_visc + coarse[x * 8 : x * 8 + 8])
            visc_s[plane * 32 + 7 : plane * 32 + 8, :] = base_visc + below_y[x : x + 1]
            visc_s[plane * 32 + 24 : plane * 32 + 25, :] = base_visc + above_y[x : x + 1]
        put(ez_s, 2 * x, base_visc + ahead[x * 8 : x * 8 + 8])
        put(ez_s, 2 * x + 1, base_visc + behind[x * 8 : x * 8 + 8])

    def plane_of(c, x):
        if x < 0:
            return vx_s[c, x + 2]
        if x > 15:
            return vx_s[c, x - 14]
        return vel[c, x]

    for x in range(16):
        vat = (x + 1) * 32
        visc = visc_s[vat + 8 : vat + 24, :]
        faces = (
            (visc_s[vat + 40 : vat + 56, :], visc_s[vat - 24 : vat - 8, :]),
            (visc_s[vat + 9 : vat + 25, :], visc_s[vat + 7 : vat + 23, :]),
            (
                ez_s[(x // 2 * 2) * 32 + 8 : (x // 2 * 2) * 32 + 24, :],
                ez_s[(x // 2 * 2 + 1) * 32 + 8 : (x // 2 * 2 + 1) * 32 + 24, :],
            ),
        )
        faces = [(0.5 * (visc + a), 0.5 * (visc + b)) for a, b in faces]
        wind = [vel[a, x] for a in range(3)]
        for c in range(3):
            u = vel[c, x]
            at = (c * 16 + x) * 32
            zat = (c * 16 + x) * 16
            zc = zcols[zat : zat + 16]
            p1 = jnp.where(lane == 127, zc[:, 0:1], pltpu.roll(u, 127, 1))
            p2 = jnp.where(lane == 127, zc[:, 1:2], jnp.where(lane == 126, zc[:, 0:1], pltpu.roll(u, 126, 1)))
            m1 = jnp.where(lane == 0, zc[:, 3:4], pltpu.roll(u, 1, 1))
            m2 = jnp.where(lane == 0, zc[:, 2:3], jnp.where(lane == 1, zc[:, 3:4], pltpu.roll(u, 2, 1)))
            near = (
                (plane_of(c, x + 1), plane_of(c, x - 1), plane_of(c, x + 2), plane_of(c, x - 2)),
                (
                    vy_s[at + 9 : at + 25, :], vy_s[at + 7 : at + 23, :],
                    vy_s[at + 10 : at + 26, :], vy_s[at + 6 : at + 22, :],
                ),
                (p1, m1, p2, m2),
            )
            advect = None
            diffuse = None
            for a in range(3):
                q1, b1, q2, b2 = near[a]
                slope = (8.0 * (q1 - b1) - (q2 - b2)) * (1.0 / 12.0)
                term = wind[a] * slope
                advect = term if advect is None else advect + term
                flux = faces[a][0] * (q1 - u) - faces[a][1] * (u - b1)
                diffuse = flux if diffuse is None else diffuse + flux
            out[c, x] = u + time_step * (diffuse - advect)


def run_flow(scal, velocity, eddy, rx_a, rx_b, ry_a, ry_b, rz):
    return pl.pallas_call(
        flow_kernel,
        out_shape=jax.ShapeDtypeStruct(velocity.shape, F32),
        in_specs=[pl.BlockSpec(memory_space=pltpu.SMEM)] + [vmem_spec()] * 7,
        out_specs=vmem_spec(),
        scratch_shapes=[
            pltpu.VMEM((3, 4, 16, 128), F32),
            pltpu.VMEM((3 * 16 * 32, 128), F32),
            pltpu.VMEM((18 * 32, 128), F32),
            pltpu.VMEM((16 * 32, 128), F32),
            pltpu.VMEM((8, 128), F32),
        ],
        compiler_params=pltpu.CompilerParams(vmem_limit_bytes=32 * 1024 * 1024),
        name="flow",
    )(scal, velocity, eddy, rx_a, rx_b, ry_a, ry_b, rz)


def finish_kernel(scal, own, blk, mine, other, loss_out, first_out, hidden_out, last_out, ext_s):
    second = scal[0, 3] == 1
    one, two = mine[...], other[...]
    top = jnp.where(second, two, one)
    bottom = jnp.where(second, one, two)
    hidden_out[0:32, :] = top[:, GRAD_AT : GRAD_AT + 27 * CH]
    hidden_out[32:64, :] = bottom[:, GRAD_AT : GRAD_AT + 27 * CH]
    ext_s[0:32, :] = top[:, 0:128]
    ext_s[32:64, :] = bottom[:, 0:128]
    extra = ext_s[...]
    first_out[...] = extra[:, 0:81]
    turned = jnp.transpose(jnp.concatenate([extra, jnp.zeros((64, 128), F32)], axis=0))
    last_out[...] = turned[LAST_COL : LAST_COL + 1, 0:64]
    slots = loss_out.shape[1]
    lane = iota((1, 128), 1)
    slot_lane = iota((1, slots), 1)
    picked = jnp.zeros((1, slots), F32)
    for s in range(slots):
        at = scal[0, 1] * slots + s
        dev = own[0, at] * scal[0, 5] + scal[0, 6]
        row = ext_s[pl.ds(dev % 64, 1), :]
        col = LOSS_COL + BLK * (dev // 64) + blk[0, at]
        value = jnp.sum(jnp.where(lane == col, row, 0.0), axis=1, keepdims=True)
        picked = jnp.where(slot_lane == s, value, picked)
    loss_out[...] = picked


def run_finish(scal, own, blk, mine, other, slots):
    smem = pl.BlockSpec(memory_space=pltpu.SMEM)
    f = lambda *s: jax.ShapeDtypeStruct(s, F32)
    return pl.pallas_call(
        finish_kernel,
        out_shape=(f(1, slots), f(64, 81), f(64, 27 * CH), f(1, 64)),
        in_specs=[smem] * 3 + [vmem_spec()] * 2,
        out_specs=tuple(vmem_spec() for _ in range(4)),
        scratch_shapes=[pltpu.VMEM((64, 128), F32)],
        name="finish",
    )(scal, own, blk, mine, other)


def on_device(velocity, target_visc, w_first, w_hidden, w_last, sample_owner, sample_block):
    n_x, n_y, n_z = lax.axis_size("gx"), lax.axis_size("gy"), lax.axis_size("role")
    trainers = n_x * n_y * n_z
    at_x, at_y, at_z = lax.axis_index("gx"), lax.axis_index("gy"), lax.axis_index("role")
    group = at_y * n_z + at_z
    half = (at_y ^ (at_y >> 1)) & 1
    scal = jnp.stack(
        [jnp.int32(trainers), at_x, at_y, half, at_x * (n_y * n_z) + group, jnp.int32(n_y * n_z), group, jnp.int32(0)]
    ).astype(jnp.int32)[None]
    own = sample_owner.reshape(1, -1)
    blk = sample_block.reshape(1, -1)
    slots = own.shape[1] // n_x

    def pairs_a(count):
        return [(i, i ^ 1) for i in range(count)]

    def pairs_b(count):
        return [(i, (i - 1) % count if i % 2 == 0 else (i + 1) % count) for i in range(count)]

    keep, send, eddy, hx_a, hx_b, hy_a, hy_b, hz = run_net(
        scal, velocity, target_visc, w_first, w_hidden, w_last.reshape(1, CH), own, blk
    )
    rx_a = lax.ppermute(hx_a, "gx", pairs_a(n_x))
    rx_b = lax.ppermute(hx_b, "gx", pairs_b(n_x))
    ry_a = lax.ppermute(hy_a, "gy", pairs_a(n_y))
    ry_b = lax.ppermute(hy_b, "gy", pairs_b(n_y))
    rz = lax.ppermute(hz, "role", pairs_a(n_z))

    total = keep + lax.ppermute(send, "gy", pairs_a(n_y))
    total = total + lax.ppermute(total, "gy", pairs_b(n_y))
    total = total + lax.ppermute(total, "role", pairs_a(n_z))
    if n_x == 4:
        steps = [pairs_a(n_x), pairs_b(n_x)]
    else:
        steps = [[(i, i ^ (1 << s)) for i in range(n_x)] for s in range(n_x.bit_length() - 1)]
    for step in steps:
        total = total + lax.ppermute(total, "gx", step)
    other = lax.ppermute(total, "gy", pairs_a(n_y))

    u_next = run_flow(scal, velocity, eddy, rx_a, rx_b, ry_a, ry_b, rz)
    losses, first, hidden, last = run_finish(scal, own, blk, total, other, slots)
    return (u_next, losses.reshape(1, 1, slots), first, hidden, last.reshape(CH))


def solution(mesh):
    return jax.shard_map(
        on_device,
        mesh=mesh,
        in_specs=(
            P(None, "gx", "gy", "role"),
            P("gx", "gy", "role"),
            P(),
            P(),
            P(),
            P("gy", "role", None, None),
            P("gy", "role", None, None),
        ),
        out_specs=(P(None, "gx", "gy", "role"), P("gy", "role", "gx"), P(), P(), P()),
        check_vma=False,
    )
```

time: 286 us -> 70.7 us (0.25); the launches traced: 282 us -> 70.4 us
  matrix products: 96.7 us -> 0 us
  local copies, waits for them, and re-layouts: 64.8 us -> 1.36 us
  blocking collectives: 54.2 us -> 0 us
  other arithmetic: 33.1 us -> 1.09 us
  waiting for transfers between devices: 0.4 us -> 26.3 us
  Pallas kernels: 0 us -> 19.8 us
  between operations: 16.9 us -> 0.77 us
  starting transfers between devices: 15.9 us -> 21.1 us
    dot_general x192 -> x0, matrix products: 96.7 us -> none  [the longest x107 55.4 us: convolve(): jnp.einsum('oc,bcn->bon', weight[:, k * inner:(k + 1) * inner], shifted(p...]
    psum x1 -> x0, blocking collectives: 38.9 us -> none  [on_device(): lax.psum((grad_first, grad_hidden, grad_last), ('gx', 'gy', 'role'))]
    reshape x11 -> x0, local copies, waits for them, and re-layouts: 31.2 us -> none  [the longest x1 27.3 us: on_device(): velocity.reshape(3, half_x, 2, half_y, 2, half_z, 2).mean(axis=(2, 4, 6))]
    ppermute x12 -> x11, waiting for transfers between devices: 0.38 us -> 26.3 us  [the longest x2 10.7 us: on_device(): total = total + lax.ppermute(total, 'gx', step)]
    pallas_call x0 -> x3, Pallas kernels: none -> 19.8 us  [the longest x1 14.7 us: run_net(): pl.pallas_call(net_kernel, out_shape=(f(32, PAY), f(32, PAY), f(64, 128),...]
    all_gather x1 -> x0, blocking collectives: 15.3 us -> none  [on_device(): piece = lax.all_gather(stacked, 'gx', axis=0, tiled=True)]
    ppermute x6 -> x0, local copies, waits for them, and re-layouts: 11 us -> none  [the longest x3 6.2 us: padded_2(): lax.ppermute(lax.slice_in_dim(block, block.shape[dim] - width, None, axis...]
    concatenate x6 -> x0, local copies, waits for them, and re-layouts: 9.68 us -> none  [the longest x4 7.99 us: padded_2(): block = jnp.concatenate([low, block, high], axis=dim)]
  transfers between devices with their start and end apart: 13 -> 11, of which waited for: 1 -> 7; matrix products, arithmetic and copies ran while one was open for 37% -> 0% of each run, Pallas kernels for 0% -> 4%
where the time goes in v1:
time: 70.7 us; the launch traced here: 70.4 us
  waiting for transfers between devices  26.3 us (37%)
  starting transfers between devices  21.1 us (30%)
  Pallas kernels  19.8 us (28%)
  local copies, waits for them, and re-layouts  1.36 us (2%)
  other arithmetic  1.09 us (2%)
  between operations  0.77 us (1%)
    pallas_call x1, Pallas kernels, run_net(): pl.pallas_call(net_kernel, out_shape=(f(32, PAY), f(32, PAY), f(64, 128),...  14.7 us
    ppermute x2, waiting for transfers between devices, on_device(): total = total + lax.ppermute(total, 'gx', step)  10.7 us
    ppermute x1, waiting for transfers between devices, on_device(): total = total + lax.ppermute(total, 'role', pairs_a(n_z))  6.26 us
    ppermute x1, waiting for transfers between devices, on_device(): total = total + lax.ppermute(total, 'gy', pairs_b(n_y))  6.03 us
    ppermute x2, starting transfers between devices, on_device(): total = total + lax.ppermute(total, 'gx', step)  5.42 us
    ppermute x1, starting transfers between devices, on_device(): rx_a = lax.ppermute(hx_a, 'gx', pairs_a(n_x))  4.88 us
    pallas_call x1, Pallas kernels, run_flow(): pl.pallas_call(flow_kernel, out_shape=jax.ShapeDtypeStruct(velocity.shape...  3.14 us
    ppermute x1, starting transfers between devices, on_device(): total = total + lax.ppermute(total, 'gy', pairs_b(n_y))  2.67 us
  transfers between devices with their start and end apart: 11, of which 7 were waited for; matrix products, arithmetic and copies ran while one was open for 0% of the time, Pallas kernels for 4%

profile of v1, /device:TPU:0, one launch (start us, length us, event | category | flops | bytes accessed | tf_op | source)
XLA Modules:
  0.0 70.4 jit_solution(3968442179955244037)
XLA Ops:
  0.6 0.6 stack.23
  1.3 14.7 %net.1 = (f32[32,1920]{1,0:T(8,128)}, f32[32,1920]{1,0:T(8,128)}, f32[64,128]{1,0:T(8,128)}, f32[104,128]{1,0:T(8,128)}, f32[104,128]{1,0:T(8,128)}, /*index=5*/...) custom-call(s32[1,8]{1,0:T(1,128)} %bitcast.11, f32[3,16,16,128]{3,2,1,0:T(8,128)} %vel.3, bf16[8,8,64]{2,1,0:T(8,128)(2,1)} %tgt.1, ...), custom_call_target="tpu_custom_call" | custom-call | tf_op jit(solution)/shard_map/net/pallas_call | solution.py:293
  15.9 0.5 collective-permute-start.5
  16.5 1.3 %collective-permute-done.5 = f32[32,1920]{1,0:T(8,128)S(1)} collective-permute-done((f32[32,1920]{1,0:T(8,128)}, f32[32,1920]{1,0:T(8,128)S(1)}, u32[]{:S(2)}, u32[]{:S(2)}) %collective-permute-start.5) | collective-permute-done | bytes 245792 | tf_op jit(solution)/shard_map/ppermute | solution.py:497
  17.8 1.0 %add.23 = f32[32,1920]{1,0:T(8,128)S(1)} add(f32[32,1920]{1,0:T(8,128)} %get-tuple-element.23, f32[32,1920]{1,0:T(8,128)S(1)} %collective-permute-done.5) | non-fusion elementwise | flops 61440 | bytes 737280 | tf_op jit(solution)/shard_map/add | solution.py:497
  18.8 2.7 %collective-permute-start.6 = (f32[32,1920]{1,0:T(8,128)S(1)}, f32[32,1920]{1,0:T(8,128)S(1)}, u32[]{:S(2)}, u32[]{:S(2)}) collective-permute-start(f32[32,1920]{1,0:T(8,128)S(1)} %add.23), channel_id=1, source_target_pairs={{0,6},{2,4},{4,2},{6,0},{1,7},{3,5},{5,3},{7,1},{8,14},{10,12},{12... | collective-permute-start | bytes 737288 | tf_op jit(solution)/shard_map/ppermute | solution.py:498
  21.5 6.0 %collective-permute-done.6 = f32[32,1920]{1,0:T(8,128)S(1)} collective-permute-done((f32[32,1920]{1,0:T(8,128)S(1)}, f32[32,1920]{1,0:T(8,128)S(1)}, u32[]{:S(2)}, u32[]{:S(2)}) %collective-permute-start.6) | collective-permute-done | bytes 245792 | tf_op jit(solution)/shard_map/ppermute | solution.py:498
  27.5 2.3 %collective-permute-start.7 = (f32[32,1920]{1,0:T(8,128)S(1)}, f32[32,1920]{1,0:T(8,128)S(1)}, u32[]{:S(2)}, u32[]{:S(2)}) collective-permute-start(f32[32,1920]{1,0:T(8,128)S(1)} %add.24), channel_id=1, source_target_pairs={{0,1},{1,0},{2,3},{3,2},{4,5},{5,4},{6,7},{7,6},{8,9},{9,8},{10,11... | collective-permute-start | bytes 737288 | tf_op jit(solution)/shard_map/ppermute | solution.py:499
  29.8 6.3 %collective-permute-done.7 = f32[32,1920]{1,0:T(8,128)S(1)} collective-permute-done((f32[32,1920]{1,0:T(8,128)S(1)}, f32[32,1920]{1,0:T(8,128)S(1)}, u32[]{:S(2)}, u32[]{:S(2)}) %collective-permute-start.7) | collective-permute-done | bytes 245792 | tf_op jit(solution)/shard_map/ppermute | solution.py:499
  36.1 1.9 %collective-permute-start.8 = (f32[32,1920]{1,0:T(8,128)S(1)}, f32[32,1920]{1,0:T(8,128)S(1)}, u32[]{:S(2)}, u32[]{:S(2)}) collective-permute-start(f32[32,1920]{1,0:T(8,128)S(1)} %add.25), channel_id=1, source_target_pairs={{0,8},{8,0},{16,24},{24,16},{1,9},{9,1},{17,25},{25,17},{2,10},{10... | collective-permute-start | bytes 737288 | tf_op jit(solution)/shard_map/ppermute | solution.py:505
  37.9 5.7 %collective-permute-done.8 = f32[32,1920]{1,0:T(8,128)S(1)} collective-permute-done((f32[32,1920]{1,0:T(8,128)S(1)}, f32[32,1920]{1,0:T(8,128)S(1)}, u32[]{:S(2)}, u32[]{:S(2)}) %collective-permute-start.8) | collective-permute-done | bytes 245792 | tf_op jit(solution)/shard_map/ppermute | solution.py:505
  43.7 0.0 copy-start
  43.7 3.6 %collective-permute-start.9 = (f32[32,1920]{1,0:T(8,128)S(1)}, f32[32,1920]{1,0:T(8,128)S(1)}, u32[]{:S(2)}, u32[]{:S(2)}) collective-permute-start(f32[32,1920]{1,0:T(8,128)S(1)} %add.26), channel_id=1, source_target_pairs={{0,24},{8,16},{16,8},{24,0},{1,25},{9,17},{17,9},{25,1},{2,26},{10... | collective-permute-start | bytes 737288 | tf_op jit(solution)/shard_map/ppermute | solution.py:505
  47.3 5.0 %collective-permute-done.9 = f32[32,1920]{1,0:T(8,128)S(1)} collective-permute-done((f32[32,1920]{1,0:T(8,128)S(1)}, f32[32,1920]{1,0:T(8,128)S(1)}, u32[]{:S(2)}, u32[]{:S(2)}) %collective-permute-start.9) | collective-permute-done | bytes 245792 | tf_op jit(solution)/shard_map/ppermute | solution.py:505
  52.3 0.1 collective-permute-start.10
  52.4 1.2 %collective-permute-start.4 = (f32[8,896]{1,0:T(8,128)S(1)}, f32[8,896]{1,0:T(8,128)S(1)}, u32[]{:S(2)}, u32[]{:S(2)}) collective-permute-start(f32[8,896]{1,0:T(8,128)S(1)} %copy-done.9), channel_id=1, source_target_pairs={{0,1},{1,0},{2,3},{3,2},{4,5},{5,4},{6,7},{7,6},{8,9},{9,8},{10,11... | collective-permute-start | bytes 86024 | tf_op jit(solution)/shard_map/ppermute | solution.py:495
  53.6 4.9 %collective-permute-start = (f32[104,128]{1,0:T(8,128)S(1)}, f32[104,128]{1,0:T(8,128)S(1)}, u32[]{:S(2)}, u32[]{:S(2)}) collective-permute-start(f32[104,128]{1,0:T(8,128)S(1)} %copy-done.8), channel_id=1, source_target_pairs={{0,8},{8,0},{16,24},{24,16},{1,9},{9,1},{17,25},{25,17},{2,10},{10... | collective-permute-start | bytes 159752 | tf_op jit(solution)/shard_map/ppermute | solution.py:491
  58.5 2.5 %collective-permute-start.1 = (f32[104,128]{1,0:T(8,128)S(1)}, f32[104,128]{1,0:T(8,128)S(1)}, u32[]{:S(2)}, u32[]{:S(2)}) collective-permute-start(f32[104,128]{1,0:T(8,128)S(1)} %copy-done.7), channel_id=1, source_target_pairs={{0,24},{8,16},{16,8},{24,0},{1,25},{9,17},{17,9},{25,1},{2,26},{10... | collective-permute-start | bytes 159752 | tf_op jit(solution)/shard_map/ppermute | solution.py:492
  61.0 1.6 %collective-permute-start.3 = (f32[104,128]{1,0:T(8,128)S(1)}, f32[104,128]{1,0:T(8,128)S(1)}, u32[]{:S(2)}, u32[]{:S(2)}) collective-permute-start(f32[104,128]{1,0:T(8,128)S(1)} %copy-done.5), channel_id=1, source_target_pairs={{0,6},{2,4},{4,2},{6,0},{1,7},{3,5},{5,3},{7,1},{8,14},{10,12},{12... | collective-permute-start | bytes 159752 | tf_op jit(solution)/shard_map/ppermute | solution.py:494
  62.7 1.8 %collective-permute-done.1.rx_b = f32[104,128]{1,0:T(8,128)S(1)} collective-permute-done((f32[104,128]{1,0:T(8,128)S(1)}, f32[104,128]{1,0:T(8,128)S(1)}, u32[]{:S(2)}, u32[]{:S(2)}) %collective-permute-start.1) | collective-permute-done | bytes 53280 | tf_op jit(solution)/shard_map/ppermute | solution.py:492
  64.4 0.2 collective-permute-done.3.ry_b
  64.6 3.1 %flow.1 = f32[3,16,16,128]{3,2,1,0:T(8,128)} custom-call(s32[1,8]{1,0:T(1,128)S(1)} %bitcast.13, f32[3,16,16,128]{3,2,1,0:T(8,128)S(1)} %copy-done, f32[64,128]{1,0:T(8,128)S(1)} %copy-done.1, f32[104,128]{1,0:T(8,128)S(1)} %collective-permute-done.rx_a, f32[104,128]{1,0:T(8,128)S(1)} %collective-permute-done.1.rx_b, ...), custom_call_target="tpu_custom_call" | custom-call | tf_op jit(solution)/shard_map/flow/pallas_call | solution.py:412
  67.8 0.7 copy-done.4
  68.5 2.0 %finish.1 = (f32[1,8]{1,0:T(1,128)}, f32[64,81]{1,0:T(8,128)}, f32[64,1728]{1,0:T(8,128)}, f32[1,64]{1,0:T(1,128)}) custom-call(s32[1,8]{1,0:T(1,128)} %bitcast.12, s32[1,32]{1,0:T(1,128)} %bitcast.15, s32[1,32]{1,0:T(1,128)} %bitcast.17, f32[32,1920]{1,0:T(8,128)} %copy-done.3, f32[32,1920]{1,0:T(8,128)} %copy-done.4), custom_call_target="tpu_custom_call" | custom-call | tf_op jit(solution)/shard_map/finish/pallas_call | solution.py:459
  (27 shorter events, 0.2 us)
Async XLA Ops:
  15.9 1.9 %collective-permute-start.5 = (f32[32,1920]{1,0:T(8,128)}, f32[32,1920]{1,0:T(8,128)S(1)}, u32[]{:S(2)}, u32[]{:S(2)}) collective-permute-start(f32[32,1920]{1,0:T(8,128)} %get-tuple-element.24), channel_id=1, source_target_pairs={{0,2},{2,0},{4,6},{6,4},{1,3},{3,1},{5,7},{7,5},{8,10},{10,8},{12,... | collective-permute-start | bytes 737288 | tf_op jit(solution)/shard_map/ppermute | solution.py:497
  18.8 8.7 %collective-permute-start.6 = (f32[32,1920]{1,0:T(8,128)S(1)}, f32[32,1920]{1,0:T(8,128)S(1)}, u32[]{:S(2)}, u32[]{:S(2)}) collective-permute-start(f32[32,1920]{1,0:T(8,128)S(1)} %add.23), channel_id=1, source_target_pairs={{0,6},{2,4},{4,2},{6,0},{1,7},{3,5},{5,3},{7,1},{8,14},{10,12},{12... | collective-permute-start | bytes 737288 | tf_op jit(solution)/shard_map/ppermute | solution.py:498
  27.5 8.5 %collective-permute-start.7 = (f32[32,1920]{1,0:T(8,128)S(1)}, f32[32,1920]{1,0:T(8,128)S(1)}, u32[]{:S(2)}, u32[]{:S(2)}) collective-permute-start(f32[32,1920]{1,0:T(8,128)S(1)} %add.24), channel_id=1, source_target_pairs={{0,1},{1,0},{2,3},{3,2},{4,5},{5,4},{6,7},{7,6},{8,9},{9,8},{10,11... | collective-permute-start | bytes 737288 | tf_op jit(solution)/shard_map/ppermute | solution.py:499
  36.1 7.6 %collective-permute-start.8 = (f32[32,1920]{1,0:T(8,128)S(1)}, f32[32,1920]{1,0:T(8,128)S(1)}, u32[]{:S(2)}, u32[]{:S(2)}) collective-permute-start(f32[32,1920]{1,0:T(8,128)S(1)} %add.25), channel_id=1, source_target_pairs={{0,8},{8,0},{16,24},{24,16},{1,9},{9,1},{17,25},{25,17},{2,10},{10... | collective-permute-start | bytes 737288 | tf_op jit(solution)/shard_map/ppermute | solution.py:505
  43.7 8.7 %copy-start.9 = (f32[8,896]{1,0:T(8,128)S(1)}, f32[8,896]{1,0:T(8,128)}, u32[]{:S(2)}) copy-start(f32[8,896]{1,0:T(8,128)} %get-tuple-element.22) | copy-start | bytes 86020
  43.7 10.0 %copy-start.8 = (f32[104,128]{1,0:T(8,128)S(1)}, f32[104,128]{1,0:T(8,128)}, u32[]{:S(2)}) copy-start(f32[104,128]{1,0:T(8,128)} %get-tuple-element.18) | copy-start | bytes 159748
  43.7 14.8 %copy-start.7 = (f32[104,128]{1,0:T(8,128)S(1)}, f32[104,128]{1,0:T(8,128)}, u32[]{:S(2)}) copy-start(f32[104,128]{1,0:T(8,128)} %get-tuple-element.19) | copy-start | bytes 159748
  43.7 17.3 %copy-start.6 = (f32[104,128]{1,0:T(8,128)S(1)}, f32[104,128]{1,0:T(8,128)}, u32[]{:S(2)}) copy-start(f32[104,128]{1,0:T(8,128)} %get-tuple-element.20) | copy-start | bytes 159748
  43.7 17.3 %copy-start.5 = (f32[104,128]{1,0:T(8,128)S(1)}, f32[104,128]{1,0:T(8,128)}, u32[]{:S(2)}) copy-start(f32[104,128]{1,0:T(8,128)} %get-tuple-element.21) | copy-start | bytes 159748
  43.7 20.9 %copy-start = (f32[3,16,16,128]{3,2,1,0:T(8,128)S(1)}, f32[3,16,16,128]{3,2,1,0:T(8,128)}, u32[]{:S(2)}) copy-start(f32[3,16,16,128]{3,2,1,0:T(8,128)} %vel.3) | copy-start | bytes 1179652
  43.7 8.6 %collective-permute-start.9 = (f32[32,1920]{1,0:T(8,128)S(1)}, f32[32,1920]{1,0:T(8,128)S(1)}, u32[]{:S(2)}, u32[]{:S(2)}) collective-permute-start(f32[32,1920]{1,0:T(8,128)S(1)} %add.26), channel_id=1, source_target_pairs={{0,24},{8,16},{16,8},{24,0},{1,25},{9,17},{17,9},{25,1},{2,26},{10... | collective-permute-start | bytes 737288 | tf_op jit(solution)/shard_map/ppermute | solution.py:505
  52.3 12.4 %copy-start.1 = (f32[64,128]{1,0:T(8,128)S(1)}, f32[64,128]{1,0:T(8,128)}, u32[]{:S(2)}) copy-start(f32[64,128]{1,0:T(8,128)} %get-tuple-element.17.eddy) | copy-start | bytes 98308
  52.3 15.5 %copy-start.3 = (f32[32,1920]{1,0:T(8,128)}, f32[32,1920]{1,0:T(8,128)S(1)}, u32[]{:S(2)}) copy-start(f32[32,1920]{1,0:T(8,128)S(1)} %add.27.mine) | copy-start | bytes 737284
  52.3 15.5 %collective-permute-start.10 = (f32[32,1920]{1,0:T(8,128)S(1)}, f32[32,1920]{1,0:T(8,128)S(1)}, u32[]{:S(2)}, u32[]{:S(2)}) collective-permute-start(f32[32,1920]{1,0:T(8,128)S(1)} %add.27.mine), channel_id=1, source_target_pairs={{0,2},{2,0},{4,6},{6,4},{1,3},{3,1},{5,7},{7,5},{8,10},{10,8},{12,... | collective-permute-start | bytes 737288 | tf_op jit(solution)/shard_map/ppermute | solution.py:506
  52.4 8.6 %collective-permute-start.4 = (f32[8,896]{1,0:T(8,128)S(1)}, f32[8,896]{1,0:T(8,128)S(1)}, u32[]{:S(2)}, u32[]{:S(2)}) collective-permute-start(f32[8,896]{1,0:T(8,128)S(1)} %copy-done.9), channel_id=1, source_target_pairs={{0,1},{1,0},{2,3},{3,2},{4,5},{5,4},{6,7},{7,6},{8,9},{9,8},{10,11... | collective-permute-start | bytes 86024 | tf_op jit(solution)/shard_map/ppermute | solution.py:495
  53.6 9.0 %collective-permute-start = (f32[104,128]{1,0:T(8,128)S(1)}, f32[104,128]{1,0:T(8,128)S(1)}, u32[]{:S(2)}, u32[]{:S(2)}) collective-permute-start(f32[104,128]{1,0:T(8,128)S(1)} %copy-done.8), channel_id=1, source_target_pairs={{0,8},{8,0},{16,24},{24,16},{1,9},{9,1},{17,25},{25,17},{2,10},{10... | collective-permute-start | bytes 159752 | tf_op jit(solution)/shard_map/ppermute | solution.py:491
  58.5 5.9 %collective-permute-start.1 = (f32[104,128]{1,0:T(8,128)S(1)}, f32[104,128]{1,0:T(8,128)S(1)}, u32[]{:S(2)}, u32[]{:S(2)}) collective-permute-start(f32[104,128]{1,0:T(8,128)S(1)} %copy-done.7), channel_id=1, source_target_pairs={{0,24},{8,16},{16,8},{24,0},{1,25},{9,17},{17,9},{25,1},{2,26},{10... | collective-permute-start | bytes 159752 | tf_op jit(solution)/shard_map/ppermute | solution.py:492
  61.0 3.5 %collective-permute-start.2 = (f32[104,128]{1,0:T(8,128)S(1)}, f32[104,128]{1,0:T(8,128)S(1)}, u32[]{:S(2)}, u32[]{:S(2)}) collective-permute-start(f32[104,128]{1,0:T(8,128)S(1)} %copy-done.6), channel_id=1, source_target_pairs={{0,2},{2,0},{4,6},{6,4},{1,3},{3,1},{5,7},{7,5},{8,10},{10,8},{12,... | collective-permute-start | bytes 159752 | tf_op jit(solution)/shard_map/ppermute | solution.py:493
  61.0 3.6 %copy-start.2 = (s32[8]{0:T(128)S(1)}, s32[8]{0:T(128)}, u32[]{:S(2)}) copy-start(s32[8]{0:T(128)} %stack.23) | copy-start | bytes 100
  61.0 3.6 %collective-permute-start.3 = (f32[104,128]{1,0:T(8,128)S(1)}, f32[104,128]{1,0:T(8,128)S(1)}, u32[]{:S(2)}, u32[]{:S(2)}) collective-permute-start(f32[104,128]{1,0:T(8,128)S(1)} %copy-done.5), channel_id=1, source_target_pairs={{0,6},{2,4},{4,2},{6,0},{1,7},{3,5},{5,3},{7,1},{8,14},{10,12},{12... | collective-permute-start | bytes 159752 | tf_op jit(solution)/shard_map/ppermute | solution.py:494
  67.8 0.7 copy-start.4

commit v2 on v1

--- a/solution.py
+++ b/solution.py
@@ -16,7 +16,6 @@
 ROWS = SIDE * SIDE * BLK
 WIDE = SIDE * CH
 SLAB = SIDE * BLK
-GRAD_AT = 128
 PAY = 1920
 LAST_COL = 81
 LOSS_COL = 82
@@ -47,8 +46,8 @@
 
 def net_kernel(
     scal, vel, tgt, w1, w2, w3, own, blk,
-    keep, send, eddy_out, hx_a, hx_b, hy_a, hy_b, hz,
-    pool_s, fp_s, i1_s, a_s, d_s, tt_s, tb_s, pre_s, slope1_s, ah_s, slope2_s, dw_s, big_s, gh_s,
+    keep, send, eddy_out, halo1, halo2, halo3, halo4,
+    hx_a, hx_b, hy_b, hz, pool_s, fp_s, i1_s, a_s, d_s, tt_s, tb_s, pre_s, slope1_s, ah_s, slope2_s, dw_s, big_s, gh_s,
 ):
     trainers = scal[0, 0]
     gx_at = scal[0, 1]
@@ -69,26 +68,26 @@
             cols.append(pool_s[c, x, pl.ds(0, 8, stride=2), :] + pool_s[c, x, pl.ds(1, 8, stride=2), :])
         rows.append(jnp.concatenate(cols, axis=0))
     pooled = jnp.concatenate(rows, axis=0)
-    zpool = jnp.where(iota((128, 64), 0) // 2 == iota((128, 64), 1), 0.125, 0.0).astype(F32)
+    zpool = jnp.where(iota((128, 1), 0) >> 1 == iota((1, 64), 1), 0.125, 0.0)
     filt = nn(pooled, zpool, HIGH).astype(BF16)
     tgt_rows = tgt[...].reshape(64, 64)
     zsel = jnp.concatenate([filt[0:64], filt[64:128], filt[128:192], tgt_rows], axis=1)
-    spread = onehot(iota((ROWS, 64), 0) // BLK == iota((ROWS, 64), 1))
+    spread = onehot(iota((ROWS, 1), 0) >> 3 == iota((1, 64), 1))
     by_block = nn(spread, zsel)
-    mine = (iota((ROWS, 256), 1) % 64) // SIDE == iota((ROWS, 256), 0) % BLK
+    mine = (iota((1, 256), 1) & 63) >> 3 == iota((ROWS, 1), 0) & 7
     by_block = jnp.where(mine, by_block, 0.0).astype(BF16)
-    src_c = iota((256, 256), 0) // 64
-    src_z = iota((256, 256), 0) % SIDE
-    dst = iota((256, 256), 1)
-    pick = onehot((dst < 216) & ((dst % 24) // SIDE == src_c) & (dst % SIDE == src_z))
+    lane_in = iota((1, 256), 1)
+    lane_off = lax.div(lane_in, 24)
+    lane_cz = lane_in - lane_off * 24
+    src = iota((256, 1), 0)
+    pick = onehot(jnp.where(lane_in < 216, lane_cz, -1) == (src >> 6) * 8 + (src & 7))
     cells = nn(by_block, pick)
-    dst8 = iota((256, SIDE), 1)
-    pick_t = onehot((iota((256, SIDE), 0) // 64 == 3) & (iota((256, SIDE), 0) % SIDE == dst8))
+    pick_t = onehot(jnp.where(src >= 192, src & 7, -1) == iota((1, SIDE), 1))
     target = nn(by_block, pick_t)
 
     fp_s[...] = jnp.zeros(fp_s.shape, F32)
     fp_s[1:9, 1:9] = cells.reshape(SIDE, SIDE, BLK, 256)
-    group = iota((1, 1, 1, 256), 3) // 24
+    group = lax.div(iota((1, 1, 1, 256), 3), 24)
     for x in range(SIDE):
         acc = jnp.zeros((1, SIDE, BLK, 256), F32)
         for k in range(9):
@@ -96,26 +95,25 @@
             acc = jnp.where(group == k, part, acc)
         i1_s[x * SLAB : (x + 1) * SLAB, :] = acc.reshape(SLAB, 256).astype(BF16)
 
-    j_at = iota((81, 256), 0)
-    l_at = iota((81, 256), 1)
-    same = (l_at < 216) & (j_at // 9 == l_at // 24) & (j_at % 3 == (l_at % 24) // SIDE)
-    delta = l_at % SIDE - ((j_at // 3) % 3 - 1)
+    j_at = iota((81, 1), 0)
+    j_off, j_dz, j_c = lax.div(j_at, 9), lax.rem(lax.div(j_at, 3), 3) - 1, lax.rem(j_at, 3)
+    lane_key = jnp.where(lane_in < 216, lane_off * 4 + (lane_cz >> 3), -1)
+    same = lane_key == j_off * 4 + j_c
+    delta = jnp.where(same, (lane_in & 7) - j_dz, -9)
     w1v = w1[...]
-    t1 = jnp.concatenate([nn(w1v, onehot(same & (delta == z))).astype(BF16) for z in range(SIDE)], axis=0)
+    t1 = jnp.concatenate([nn(w1v, onehot(delta == z)).astype(BF16) for z in range(SIDE)], axis=0)
     pre_s[...] = nt(i1_s[...], t1)
 
-    src = iota((256, 512), 0)
-    dst = iota((256, 512), 1)
-    d_of = dst // 128 - 2
-    half_of = (dst % 128) // 64
+    src = iota((320, 1), 0) - 64
+    dst = iota((1, 512), 1)
+    wanted = ((dst >> 7) - 2 + ((dst & 127) >> 6)) * 64 + (dst & 63)
+    chooser = onehot(jnp.where((src >= 0) & (src < 192), src - 64, -999) == wanted)
     zero_tile = jnp.zeros((64, 128), BF16)
     for k in range(9):
         base = (192 * k) // 128 * 128
         off = 192 * k - base
         width = min(256, 1728 - base)
-        rel = src - off
-        chooser = onehot((rel >= 0) & (rel < 192) & (rel // 64 - 1 == d_of + half_of) & (rel % 64 == dst % 64))
-        tiles = nn(w2[:, base : base + width], chooser[:width]).astype(BF16)
+        tiles = nn(w2[:, base : base + width], chooser[64 - off : 64 - off + width]).astype(BF16)
         ks, js = k // 3, k % 3
         kb, jb = (8 - k) // 3, (8 - k) % 3
         for z in range(SIDE):
@@ -151,18 +149,19 @@
         slope2_s[x * SLAB : (x + 1) * SLAB, :] = sig * (1.0 + pre * (1.0 - sig))
         ah_s[x * SLAB : (x + 1) * SLAB, :] = (pre * sig).astype(BF16)
 
-    tile8 = onehot(iota((64, WIDE), 0) == iota((64, WIDE), 1) % 64)
+    tile8 = onehot(iota((64, 1), 0) == iota((1, WIDE), 1) & 63)
     w3_wide = nn(w3[...], tile8)
-    last = jnp.where(iota((SIDE, WIDE), 1) // 64 == iota((SIDE, WIDE), 0), w3_wide, 0.0).astype(BF16)
+    diag = iota((1, WIDE), 1) >> 6 == iota((SIDE, 1), 0)
+    last = jnp.where(diag, w3_wide, 0.0).astype(BF16)
     logits = nt(ah_s[...], last)
     eddy = 0.5 * (jnp.maximum(logits, 0.0) + jnp.log1p(jnp.exp(-jnp.abs(logits))))
     error = eddy - target
     losses = jnp.sum(jnp.sum((error * error).reshape(64, BLK, SIDE), axis=0), axis=1, keepdims=True) / CELLS
     d_logit = (error * jax.nn.sigmoid(logits) / (trainers.astype(F32) * CELLS)).astype(BF16)
 
-    zrep = onehot(iota((SIDE, 128), 0) == (iota((SIDE, 128), 1) % 16) // 2, F32)
+    zrep = onehot(iota((SIDE, 1), 0) == (iota((1, 128), 1) & 15) >> 1, F32)
     fine = nn(eddy, zrep, HIGH)
-    fine = jnp.where(iota((ROWS, 128), 1) // 16 == iota((ROWS, 128), 0) % BLK, fine, 0.0)
+    fine = jnp.where(iota((1, 128), 1) >> 4 == iota((ROWS, 1), 0) & 7, fine, 0.0)
     fine = jnp.sum(fine.reshape(64, BLK, 128), axis=1)
     eddy_out[...] = fine
 
@@ -174,24 +173,31 @@
             hx_b[at : at + 16, :] = jnp.where(gx_odd, hi, lo)
     hx_a[96:104, :] = jnp.where(gx_odd, fine[0:8], fine[56:64])
     hx_b[96:104, :] = jnp.where(gx_odd, fine[56:64], fine[0:8])
+    core = send.at[480:584]
     for c in range(3):
         for i in range(2):
             lo = jnp.concatenate([vel[c, x, i : i + 1, :] for x in range(16)], axis=0)
             hi = jnp.concatenate([vel[c, x, 14 + i : 15 + i, :] for x in range(16)], axis=0)
             at = (c * 2 + i) * 16
-            hy_a[at : at + 16, :] = jnp.where(gy_odd, lo, hi)
+            core[at : at + 16, :] = jnp.where(gy_odd, lo, hi)
             hy_b[at : at + 16, :] = jnp.where(gy_odd, hi, lo)
     lo = eddy_out[pl.ds(0, 8, stride=8), :]
     hi = eddy_out[pl.ds(7, 8, stride=8), :]
-    hy_a[96:104, :] = jnp.where(gy_odd, lo, hi)
+    core[96:104, :] = jnp.where(gy_odd, lo, hi)
     hy_b[96:104, :] = jnp.where(gy_odd, hi, lo)
     vt = jnp.transpose(vel[...].reshape(768, 128))
+    et = jnp.transpose(jnp.concatenate([fine, jnp.zeros((64, 128), F32)], axis=0))
     hz[...] = jnp.zeros(hz.shape, F32)
-    hz[0:2, 0:768] = vt[0:2]
-    hz[2:4, 0:768] = vt[126:128]
-    et = jnp.transpose(jnp.concatenate([fine, jnp.zeros((64, 128), F32)], axis=0))
-    hz[0:1, 768:896] = et[0:1]
-    hz[1:2, 768:896] = et[127:128]
+    for t in range(6):
+        hz[t * 8 : t * 8 + 2, :] = vt[0:2, t * 128 : (t + 1) * 128]
+        hz[t * 8 + 2 : t * 8 + 4, :] = vt[126:128, t * 128 : (t + 1) * 128]
+    hz[48:49, :] = et[0:1]
+    hz[49:50, :] = et[127:128]
+    second = half == 1
+    halo1[...] = jnp.where(second, hx_a[...], hy_b[...])
+    halo2[...] = jnp.where(second, hy_b[...], hz[...])
+    halo3[...] = jnp.where(second, hx_b[...], hx_a[...])
+    halo4[...] = jnp.where(second, hz[...], hx_b[...])
 
     code = own[...] * BLK + blk[...]
     listed = code.shape[1]
@@ -242,7 +248,7 @@
     d1_lo = (d1t - d1_hi.astype(F32)).astype(BF16)
     i1 = i1_s[...]
     g1 = nn(d1_hi, i1) + nn(d1_lo, i1)
-    z_in = iota((64, 256), 1) % SIDE
+    z_in = iota((1, 256), 1) & 7
     parts = []
     for dz in (-1, 0, 1):
         tot = jnp.zeros((64, 256), F32)
@@ -250,14 +256,12 @@
             if 0 <= z + dz < SIDE:
                 tot = tot + jnp.where(z_in == z + dz, g1[z * 64 : (z + 1) * 64], 0.0)
         parts.append(tot)
-    r_at = iota((768, 128), 0)
-    c_at = iota((768, 128), 1)
-    l_at = r_at % 256
-    fold = onehot(
-        (l_at < 216) & (c_at // 9 == l_at // 24) & ((c_at // 3) % 3 == r_at // 256) & (c_at % 3 == (l_at % 24) // SIDE)
-        & (c_at < 81),
-        F32,
-    )
+    r_at = iota((768, 1), 0)
+    c_at = iota((1, 128), 1)
+    r_lane = r_at & 255
+    r_off = lax.div(r_lane, 24)
+    r_col = (r_off * 3 + (r_at >> 8)) * 3 + ((r_lane - r_off * 24) >> 3)
+    fold = onehot(jnp.where(r_lane < 216, r_col, -1) == c_at, F32)
     g_first = nn(jnp.concatenate(parts, axis=1), fold, HIGH)
 
     dlw = d_logit.astype(F32) * count_rows
@@ -265,8 +269,8 @@
     dl_lo = (dlw - dl_hi.astype(F32)).astype(BF16)
     ah = ah_s[...]
     gl = tn(dl_hi, ah) + tn(dl_lo, ah)
-    gl = jnp.where(iota((SIDE, WIDE), 1) // 64 == iota((SIDE, WIDE), 0), gl, 0.0)
-    fold_o = onehot(iota((64, WIDE), 1) % 64 == iota((64, WIDE), 0), F32)
+    gl = jnp.where(diag, gl, 0.0)
+    fold_o = onehot(iota((1, WIDE), 1) & 63 == iota((64, 1), 0), F32)
     g_last = jnp.sum(nt(fold_o, gl, HIGH), axis=1, keepdims=True)
 
     lane8 = iota((BLK, 128), 1)
@@ -276,12 +280,13 @@
     extra = jnp.where(lane == LAST_COL, g_last, g_first)
     extra = extra + jnp.where(iota((64, 128), 0) == dev % 64, loss_row, 0.0)
 
-    second = half == 1
-    keep[:, 0:128] = jnp.where(second, extra[32:64], extra[0:32])
-    send[:, 0:128] = jnp.where(second, extra[0:32], extra[32:64])
-    top, bottom = gh_s[0:32, :], gh_s[32:64, :]
-    keep[:, 128:PAY] = jnp.where(second, bottom, top)
-    send[:, 128:PAY] = jnp.where(second, top, bottom)
+    for t in range(PAY // 128):
+        if t == 0:
+            top, bottom = extra[0:32], extra[32:64]
+        else:
+            top, bottom = (gh_s[r : r + 32, (t - 1) * 128 : t * 128] for r in (0, 32))
+        keep[t * 32 : (t + 1) * 32, :] = jnp.where(second, bottom, top)
+        send[t * 32 : (t + 1) * 32, :] = jnp.where(second, top, bottom)
 
 
 def vmem_spec():
@@ -292,10 +297,14 @@
     f = lambda *s: jax.ShapeDtypeStruct(s, F32)
     return pl.pallas_call(
         net_kernel,
-        out_shape=(f(32, PAY), f(32, PAY), f(64, 128), f(104, 128), f(104, 128), f(104, 128), f(104, 128), f(8, 896)),
+        out_shape=(f(480, 128), f(584, 128), f(64, 128)) + (f(104, 128),) * 4,
         in_specs=[pl.BlockSpec(memory_space=pltpu.SMEM)] + [vmem_spec()] * 7,
-        out_specs=tuple(vmem_spec() for _ in range(8)),
+        out_specs=tuple(vmem_spec() for _ in range(7)),
         scratch_shapes=[
+            pltpu.VMEM((104, 128), F32),
+            pltpu.VMEM((104, 128), F32),
+            pltpu.VMEM((104, 128), F32),
+            pltpu.VMEM((104, 128), F32),
             pltpu.VMEM((3, SIDE, 16, 128), F32),
             pltpu.VMEM((10, 10, BLK, 256), F32),
             pltpu.VMEM((ROWS, 256), BF16),
@@ -316,9 +325,17 @@
     )(scal, velocity, target, w1, w2, w3, own, blk)
 
 
-def flow_kernel(scal, vel, eddy, rx_a, rx_b, ry_a, ry_b, rz, out, vx_s, vy_s, visc_s, ez_s, fine_s):
+def flow_kernel(
+    scal, vel, eddy, got0, got1, got2, got3, got4, out, rx_a, rx_b, ry_a, ry_b, rz, vx_s, vy_s, visc_s, ez_s
+):
     gx_odd = scal[0, 1] % 2 == 1
     gy_odd = scal[0, 2] % 2 == 1
+    second = scal[0, 3] == 1
+    ry_a[...] = got0[...]
+    ry_b[...] = jnp.where(second, got2[...], got1[...])
+    rx_a[...] = jnp.where(second, got1[...], got3[...])
+    rx_b[...] = jnp.where(second, got3[...], got4[...])
+    rz[...] = jnp.where(second, got4[...], got2[...])
     lane = iota((1, 128), 1)
 
     def sides(odd, a, b, at, rows):
@@ -336,7 +353,7 @@
             vx_s[c, i] = below
             vx_s[c, 2 + i] = above
 
-    zcols = jnp.transpose(rz[...])
+    zcols = jnp.concatenate([jnp.transpose(rz[t * 8 : t * 8 + 8, :]) for t in range(7)], axis=0)
     coarse = eddy[...]
     e_first, e_last = zcols[768:832, 0:1], zcols[768:832, 1:2]
     ahead = jnp.where(lane == 127, e_first, pltpu.roll(coarse, 127, 1))
@@ -408,33 +425,41 @@
             out[c, x] = u + time_step * (diffuse - advect)
 
 
-def run_flow(scal, velocity, eddy, rx_a, rx_b, ry_a, ry_b, rz):
+def run_flow(scal, velocity, eddy, *got):
     return pl.pallas_call(
         flow_kernel,
         out_shape=jax.ShapeDtypeStruct(velocity.shape, F32),
         in_specs=[pl.BlockSpec(memory_space=pltpu.SMEM)] + [vmem_spec()] * 7,
         out_specs=vmem_spec(),
         scratch_shapes=[
+            pltpu.VMEM((104, 128), F32),
+            pltpu.VMEM((104, 128), F32),
+            pltpu.VMEM((104, 128), F32),
+            pltpu.VMEM((104, 128), F32),
+            pltpu.VMEM((104, 128), F32),
             pltpu.VMEM((3, 4, 16, 128), F32),
             pltpu.VMEM((3 * 16 * 32, 128), F32),
             pltpu.VMEM((18 * 32, 128), F32),
             pltpu.VMEM((16 * 32, 128), F32),
-            pltpu.VMEM((8, 128), F32),
         ],
         compiler_params=pltpu.CompilerParams(vmem_limit_bytes=32 * 1024 * 1024),
         name="flow",
-    )(scal, velocity, eddy, rx_a, rx_b, ry_a, ry_b, rz)
+    )(scal, velocity, eddy, *got)
 
 
 def finish_kernel(scal, own, blk, mine, other, loss_out, first_out, hidden_out, last_out, ext_s):
     second = scal[0, 3] == 1
-    one, two = mine[...], other[...]
-    top = jnp.where(second, two, one)
-    bottom = jnp.where(second, one, two)
-    hidden_out[0:32, :] = top[:, GRAD_AT : GRAD_AT + 27 * CH]
-    hidden_out[32:64, :] = bottom[:, GRAD_AT : GRAD_AT + 27 * CH]
-    ext_s[0:32, :] = top[:, 0:128]
-    ext_s[32:64, :] = bottom[:, 0:128]
+    for t in range(PAY // 128):
+        one, two = mine[t * 32 : (t + 1) * 32, :], other[t * 32 : (t + 1) * 32, :]
+        top, bottom = jnp.where(second, two, one), jnp.where(second, one, two)
+        if t == 0:
+            ext_s[0:32, :] = top
+            ext_s[32:64, :] = bottom
+        else:
+            at = (t - 1) * 128
+            width = min(128, 27 * CH - at)
+            hidden_out[0:32, at : at + width] = top[:, :width]
+            hidden_out[32:64, at : at + width] = bottom[:, :width]
     extra = ext_s[...]
     first_out[...] = extra[:, 0:81]
     turned = jnp.transpose(jnp.concatenate([extra, jnp.zeros((64, 128), F32)], axis=0))
@@ -462,6 +487,7 @@
         in_specs=[smem] * 3 + [vmem_spec()] * 2,
         out_specs=tuple(vmem_spec() for _ in range(4)),
         scratch_shapes=[pltpu.VMEM((64, 128), F32)],
+        compiler_params=pltpu.CompilerParams(vmem_limit_bytes=32 * 1024 * 1024),
         name="finish",
     )(scal, own, blk, mine, other)
 
@@ -479,33 +505,57 @@
     blk = sample_block.reshape(1, -1)
     slots = own.shape[1] // n_x
 
-    def pairs_a(count):
-        return [(i, i ^ 1) for i in range(count)]
-
-    def pairs_b(count):
-        return [(i, (i - 1) % count if i % 2 == 0 else (i + 1) % count) for i in range(count)]
-
-    keep, send, eddy, hx_a, hx_b, hy_a, hy_b, hz = run_net(
+    axes = ("gx", "gy", "role")
+
+    def even_odd(i, count):
+        return i ^ 1
+
+    def odd_even(i, count):
+        return (i - 1) % count if i % 2 == 0 else (i + 1) % count
+
+    def partner(kind, i, j, r):
+        if kind == "x":
+            j = odd_even(j, n_y)
+        elif kind == "y":
+            r = r ^ 1
+        elif kind == "z_a":
+            i = even_odd(i, n_x)
+        else:
+            i = odd_even(i, n_x)
+        return (i * n_y + j) * n_z + r
+
+    def mixed(kinds):
+        pairs = []
+        for i in range(n_x):
+            for j in range(n_y):
+                for r in range(n_z):
+                    pairs.append(((i * n_y + j) * n_z + r, partner(kinds[(j ^ (j >> 1)) & 1], i, j, r)))
+        return pairs
+
+    core_pairs = [(j, even_odd(j, n_y)) for j in range(n_y)]
+    size = PAY // 4
+
+    keep, send, eddy, *halos = run_net(
         scal, velocity, target_visc, w_first, w_hidden, w_last.reshape(1, CH), own, blk
     )
-    rx_a = lax.ppermute(hx_a, "gx", pairs_a(n_x))
-    rx_b = lax.ppermute(hx_b, "gx", pairs_b(n_x))
-    ry_a = lax.ppermute(hy_a, "gy", pairs_a(n_y))
-    ry_b = lax.ppermute(hy_b, "gy", pairs_b(n_y))
-    rz = lax.ppermute(hz, "role", pairs_a(n_z))
-
-    total = keep + lax.ppermute(send, "gy", pairs_a(n_y))
-    total = total + lax.ppermute(total, "gy", pairs_b(n_y))
-    total = total + lax.ppermute(total, "role", pairs_a(n_z))
-    if n_x == 4:
-        steps = [pairs_a(n_x), pairs_b(n_x)]
-    else:
-        steps = [[(i, i ^ (1 << s)) for i in range(n_x)] for s in range(n_x.bit_length() - 1)]
-    for step in steps:
-        total = total + lax.ppermute(total, "gx", step)
-    other = lax.ppermute(total, "gy", pairs_a(n_y))
-
-    u_next = run_flow(scal, velocity, eddy, rx_a, rx_b, ry_a, ry_b, rz)
+    got = lax.ppermute(send, "gy", core_pairs)
+    total = keep + got[:size]
+    rims = [got[size:]]
+    orders = (("x", "y", "z_a", "z_b"), ("z_a", "x", "z_b", "y"))
+    for s in range(4):
+        kinds = (orders[0][s], orders[1][s])
+        got = lax.ppermute(jnp.concatenate([total, halos[s]], axis=0), axes, mixed(kinds))
+        part = got[:size]
+        if n_x != 4 and "z_b" in kinds:
+            part = jnp.where(half == kinds.index("z_b"), 0.0, part)
+        total = total + part
+        rims.append(got[size:])
+    if n_x != 4:
+        for bit in range(1, n_x.bit_length() - 1):
+            total = total + lax.ppermute(total, "gx", [(i, i ^ (1 << bit)) for i in range(n_x)])
+    other = lax.ppermute(total, "gy", core_pairs)
+
+    u_next = run_flow(scal, velocity, eddy, *rims)
     losses, first, hidden, last = run_finish(scal, own, blk, total, other, slots)
     return (u_next, losses.reshape(1, 1, slots), first, hidden, last.reshape(CH))
 

time: 70.7 us -> 58.5 us (0.83); the launches traced: 70.4 us -> 57.5 us
  starting transfers between devices: 21.1 us -> 12.1 us
  waiting for transfers between devices: 26.3 us -> 22.9 us
  Pallas kernels: 19.8 us -> 19 us
    ppermute x11 -> x6, starting transfers between devices: 21.1 us -> 12.1 us  [the longest x4 11.6 us: on_device(): lax.ppermute(jnp.concatenate([total, halos[s]], axis=0), axes, mixed(kinds))]
    ppermute x11 -> x6, waiting for transfers between devices: 26.3 us -> 22.9 us  [the longest x4 21.5 us: on_device(): lax.ppermute(jnp.concatenate([total, halos[s]], axis=0), axes, mixed(kinds))]
  transfers between devices with their start and end apart: 11 -> 6, of which waited for: 7 -> 5; matrix products, arithmetic and copies ran while one was open for 0% -> 0% of each run, Pallas kernels for 4% -> 5%
where the time goes in v2:
time: 58.5 us; the launch traced here: 57.5 us
  waiting for transfers between devices  22.9 us (39%)
  Pallas kernels  19 us (32%)
  starting transfers between devices  12.1 us (21%)
  local copies, waits for them, and re-layouts  1.48 us (3%)
  other arithmetic  1.2 us (2%)
  between operations  0.83 us (1%)
    ppermute x4, waiting for transfers between devices, on_device(): lax.ppermute(jnp.concatenate([total, halos[s]], axis=0), axes, mixed(kinds))  21.5 us
    pallas_call x1, Pallas kernels, run_net(): pl.pallas_call(net_kernel, out_shape=(f(480, 128), f(584, 128), f(64, 128...  14.5 us
    ppermute x4, starting transfers between devices, on_device(): lax.ppermute(jnp.concatenate([total, halos[s]], axis=0), axes, mixed(kinds))  11.6 us
    pallas_call x1, Pallas kernels, run_flow(): pl.pallas_call(flow_kernel, out_shape=jax.ShapeDtypeStruct(velocity.shape...  3.13 us
    pallas_call x1, Pallas kernels, run_finish(): pl.pallas_call(finish_kernel, out_shape=(f(1, slots), f(64, 81), f(64, 27...  1.44 us
    ppermute x1, waiting for transfers between devices, on_device(): got = lax.ppermute(send, 'gy', core_pairs)  1.43 us
  transfers between devices with their start and end apart: 6, of which 5 were waited for; matrix products, arithmetic and copies ran while one was open for 0% of the time, Pallas kernels for 5%

profile of v2, /device:TPU:0, one launch (start us, length us, event | category | flops | bytes accessed | tf_op | source)
XLA Modules:
  0.0 57.5 jit_solution(7727866879451352137)
XLA Ops:
  0.6 0.6 %stack.23 = s32[8]{0:T(128)} concatenate(s32[1]{0:T(128)} %constant.8.clone.1, s32[1]{0:T(128)} %bitcast, s32[1]{0:T(128)} %bitcast.1, s32[1]{0:T(128)} %bitcast.2, s32[1]{0:T(128)} %bitcast.3, s32[1]{0:T(128)} %constant.21.clone.1, s32[1]{0:T(128)} %bitcast.4, s32[1]{0:T(128)} %constant.22.clone.1), dimensions={0} | concatenate | bytes 64 | tf_op jit(solution)/shard_map/stack | solution.py:501
  1.2 14.5 %net.1 = (f32[480,128]{1,0:T(8,128)}, f32[584,128]{1,0:T(8,128)}, f32[64,128]{1,0:T(8,128)}, f32[104,128]{1,0:T(8,128)}, f32[104,128]{1,0:T(8,128)}, /*index=5*/f32[104,128]{1,0:T(8,128)}, f32[104,128]{1,0:T(8,128)}) custom-call(s32[1,8]{1,0:T(1,128)} %bitcast.11, f32[3,16,16,128]{3,2,1,0:T(8,128)} %vel.3, bf16[8,8,64]{2,1,0:T(8,128)(2,1)} %tgt.1, ...), custom_call_target="tpu_custom_call" | custom-call | tf_op jit(solution)/shard_map/net/pallas_call | solution.py:298
  15.7 0.5 collective-permute-start
  16.2 1.4 %collective-permute-done = f32[584,128]{1,0:T(8,128)S(1)} collective-permute-done((f32[584,128]{1,0:T(8,128)}, f32[584,128]{1,0:T(8,128)S(1)}, u32[]{:S(2)}, u32[]{:S(2)}) %collective-permute-start) | collective-permute-done | bytes 299040 | tf_op jit(solution)/shard_map/ppermute | solution.py:541
  17.6 1.0 %slice_add_fusion.4 = f32[480,128]{1,0:T(8,128)S(1)} fusion(f32[480,128]{1,0:T(8,128)} %get-tuple-element.18, f32[584,128]{1,0:T(8,128)S(1)} %collective-permute-done), kind=kLoop, calls=%fused_computation.8 | loop fusion | flops 61440 | bytes 737280 | tf_op jit(solution)/shard_map/add | solution.py:542
  18.6 0.0 copy-done.8
  18.6 0.0 copy-start.7
  18.6 2.7 %collective-permute-start.1 = (f32[584,128]{1,0:T(8,128)S(1)}, f32[584,128]{1,0:T(8,128)S(1)}, u32[]{:S(2)}, u32[]{:S(2)}) collective-permute-start(f32[584,128]{1,0:T(8,128)S(1)} %pad_maximum_fusion), channel_id=1, source_target_pairs={{0,6},{1,7},{2,10},{3,11},{4,12},{5,13},{6,0},{7,1},{8,14},{9,15},... | collective-permute-start | bytes 897032 | tf_op jit(solution)/shard_map/ppermute | solution.py:547
  21.3 4.5 %collective-permute-done.1 = f32[584,128]{1,0:T(8,128)S(1)} collective-permute-done((f32[584,128]{1,0:T(8,128)S(1)}, f32[584,128]{1,0:T(8,128)S(1)}, u32[]{:S(2)}, u32[]{:S(2)}) %collective-permute-start.1) | collective-permute-done | bytes 299040 | tf_op jit(solution)/shard_map/ppermute | solution.py:547
  25.8 2.1 %collective-permute-start.2 = (f32[584,128]{1,0:T(8,128)S(1)}, f32[584,128]{1,0:T(8,128)S(1)}, u32[]{:S(2)}, u32[]{:S(2)}) collective-permute-start(f32[584,128]{1,0:T(8,128)S(1)} %pad_maximum_fusion.1), channel_id=1, source_target_pairs={{0,1},{1,0},{2,4},{3,5},{4,2},{5,3},{6,7},{7,6},{8,9},{9,8},{10,12... | collective-permute-start | bytes 897032 | tf_op jit(solution)/shard_map/ppermute | solution.py:547
  27.9 4.7 %collective-permute-done.2 = f32[584,128]{1,0:T(8,128)S(1)} collective-permute-done((f32[584,128]{1,0:T(8,128)S(1)}, f32[584,128]{1,0:T(8,128)S(1)}, u32[]{:S(2)}, u32[]{:S(2)}) %collective-permute-start.2) | collective-permute-done | bytes 299040 | tf_op jit(solution)/shard_map/ppermute | solution.py:547
  32.8 2.1 %collective-permute-start.3 = (f32[584,128]{1,0:T(8,128)S(1)}, f32[584,128]{1,0:T(8,128)S(1)}, u32[]{:S(2)}, u32[]{:S(2)}) collective-permute-start(f32[584,128]{1,0:T(8,128)S(1)} %pad_maximum_fusion.2), channel_id=1, source_target_pairs={{0,8},{1,9},{2,26},{3,27},{4,28},{5,29},{6,14},{7,15},{8,0},{9,1},... | collective-permute-start | bytes 897032 | tf_op jit(solution)/shard_map/ppermute | solution.py:547
  34.9 7.4 %collective-permute-done.3 = f32[584,128]{1,0:T(8,128)S(1)} collective-permute-done((f32[584,128]{1,0:T(8,128)S(1)}, f32[584,128]{1,0:T(8,128)S(1)}, u32[]{:S(2)}, u32[]{:S(2)}) %collective-permute-start.3) | collective-permute-done | bytes 299040 | tf_op jit(solution)/shard_map/ppermute | solution.py:547
  42.4 4.7 %collective-permute-start.4 = (f32[584,128]{1,0:T(8,128)S(1)}, f32[584,128]{1,0:T(8,128)S(1)}, u32[]{:S(2)}, u32[]{:S(2)}) collective-permute-start(f32[584,128]{1,0:T(8,128)S(1)} %pad_maximum_fusion.3), channel_id=1, source_target_pairs={{0,24},{1,25},{2,3},{3,2},{4,5},{5,4},{6,30},{7,31},{8,16},{9,17},... | collective-permute-start | bytes 897032 | tf_op jit(solution)/shard_map/ppermute | solution.py:547
  47.0 4.9 %collective-permute-done.4 = f32[584,128]{1,0:T(8,128)S(1)} collective-permute-done((f32[584,128]{1,0:T(8,128)S(1)}, f32[584,128]{1,0:T(8,128)S(1)}, u32[]{:S(2)}, u32[]{:S(2)}) %collective-permute-start.4) | collective-permute-done | bytes 299040 | tf_op jit(solution)/shard_map/ppermute | solution.py:547
  51.9 0.0 copy-start
  51.9 0.1 collective-permute-start.5
  52.1 0.0 copy-start.1
  52.1 0.8 %copy-done = f32[3,16,16,128]{3,2,1,0:T(8,128)S(1)} copy-done((f32[3,16,16,128]{3,2,1,0:T(8,128)S(1)}, f32[3,16,16,128]{3,2,1,0:T(8,128)}, u32[]{:S(2)}) %copy-start) | copy-done | bytes 393240
  52.9 0.0 copy-done.2
  52.9 3.1 %flow.1 = f32[3,16,16,128]{3,2,1,0:T(8,128)} custom-call(s32[1,8]{1,0:T(1,128)S(1)} %bitcast.12, f32[3,16,16,128]{3,2,1,0:T(8,128)S(1)} %copy-done, f32[64,128]{1,0:T(8,128)S(1)} %copy-done.1, f32[104,128]{1,0:T(8,128)S(1)} %slice.40.got0, f32[104,128]{1,0:T(8,128)S(1)} %slice.42.got1, f32[104,128]{1,0:T(8,128)S(1)} %slice.44.got2, ...), custom_call_target="tpu_custom_call" | custom-call | tf_op jit(solution)/shard_map/flow/pallas_call | solution.py:429
  56.1 0.0 collective-permute-done.5.other
  56.1 0.0 copy-done.3
  56.1 1.4 %finish.1 = (f32[1,8]{1,0:T(1,128)}, f32[64,81]{1,0:T(8,128)}, f32[64,1728]{1,0:T(8,128)}, f32[1,64]{1,0:T(1,128)}) custom-call(s32[1,8]{1,0:T(1,128)S(1)} %bitcast.13, s32[1,32]{1,0:T(1,128)S(1)} %bitcast.15, s32[1,32]{1,0:T(1,128)S(1)} %bitcast.17, f32[480,128]{1,0:T(8,128)S(1)} %slice_add_fusion.mine, f32[480,128]{1,0:T(8,128)S(1)} %collective-permute-done.5.other), custom_call_target="tpu_custom_call" | custom-call | tf_op jit(solution)/shard_map/finish/pallas_call | solution.py:484
  (24 shorter events, 0.3 us)
Async XLA Ops:
  15.7 1.9 %collective-permute-start = (f32[584,128]{1,0:T(8,128)}, f32[584,128]{1,0:T(8,128)S(1)}, u32[]{:S(2)}, u32[]{:S(2)}) collective-permute-start(f32[584,128]{1,0:T(8,128)} %get-tuple-element.17), channel_id=1, source_target_pairs={{0,2},{2,0},{4,6},{6,4},{1,3},{3,1},{5,7},{7,5},{8,10},{10,8},{12,... | collective-permute-start | bytes 897032 | tf_op jit(solution)/shard_map/ppermute | solution.py:541
  17.6 1.0 %copy-start.8 = (f32[104,128]{1,0:T(8,128)S(1)}, f32[104,128]{1,0:T(8,128)}, u32[]{:S(2)}) copy-start(f32[104,128]{1,0:T(8,128)} %get-tuple-element.19) | copy-start | bytes 159748
  18.6 7.2 %copy-start.7 = (f32[104,128]{1,0:T(8,128)S(1)}, f32[104,128]{1,0:T(8,128)}, u32[]{:S(2)}) copy-start(f32[104,128]{1,0:T(8,128)} %get-tuple-element.20) | copy-start | bytes 159748
  18.6 7.1 %collective-permute-start.1 = (f32[584,128]{1,0:T(8,128)S(1)}, f32[584,128]{1,0:T(8,128)S(1)}, u32[]{:S(2)}, u32[]{:S(2)}) collective-permute-start(f32[584,128]{1,0:T(8,128)S(1)} %pad_maximum_fusion), channel_id=1, source_target_pairs={{0,6},{1,7},{2,10},{3,11},{4,12},{5,13},{6,0},{7,1},{8,14},{9,15},... | collective-permute-start | bytes 897032 | tf_op jit(solution)/shard_map/ppermute | solution.py:547
  25.8 6.9 %copy-start.6 = (f32[104,128]{1,0:T(8,128)S(1)}, f32[104,128]{1,0:T(8,128)}, u32[]{:S(2)}) copy-start(f32[104,128]{1,0:T(8,128)} %get-tuple-element.21) | copy-start | bytes 159748
  25.8 6.8 %collective-permute-start.2 = (f32[584,128]{1,0:T(8,128)S(1)}, f32[584,128]{1,0:T(8,128)S(1)}, u32[]{:S(2)}, u32[]{:S(2)}) collective-permute-start(f32[584,128]{1,0:T(8,128)S(1)} %pad_maximum_fusion.1), channel_id=1, source_target_pairs={{0,1},{1,0},{2,4},{3,5},{4,2},{5,3},{6,7},{7,6},{8,9},{9,8},{10,12... | collective-permute-start | bytes 897032 | tf_op jit(solution)/shard_map/ppermute | solution.py:547
  32.7 9.6 %copy-start.5 = (f32[104,128]{1,0:T(8,128)S(1)}, f32[104,128]{1,0:T(8,128)}, u32[]{:S(2)}) copy-start(f32[104,128]{1,0:T(8,128)} %get-tuple-element.22) | copy-start | bytes 159748
  32.8 9.6 %collective-permute-start.3 = (f32[584,128]{1,0:T(8,128)S(1)}, f32[584,128]{1,0:T(8,128)S(1)}, u32[]{:S(2)}, u32[]{:S(2)}) collective-permute-start(f32[584,128]{1,0:T(8,128)S(1)} %pad_maximum_fusion.2), channel_id=1, source_target_pairs={{0,8},{1,9},{2,26},{3,27},{4,28},{5,29},{6,14},{7,15},{8,0},{9,1},... | collective-permute-start | bytes 897032 | tf_op jit(solution)/shard_map/ppermute | solution.py:547
  42.4 9.5 %collective-permute-start.4 = (f32[584,128]{1,0:T(8,128)S(1)}, f32[584,128]{1,0:T(8,128)S(1)}, u32[]{:S(2)}, u32[]{:S(2)}) collective-permute-start(f32[584,128]{1,0:T(8,128)S(1)} %pad_maximum_fusion.3), channel_id=1, source_target_pairs={{0,24},{1,25},{2,3},{3,2},{4,5},{5,4},{6,30},{7,31},{8,16},{9,17},... | collective-permute-start | bytes 897032 | tf_op jit(solution)/shard_map/ppermute | solution.py:547
  51.9 1.0 %copy-start = (f32[3,16,16,128]{3,2,1,0:T(8,128)S(1)}, f32[3,16,16,128]{3,2,1,0:T(8,128)}, u32[]{:S(2)}) copy-start(f32[3,16,16,128]{3,2,1,0:T(8,128)} %vel.3) | copy-start | bytes 1179652
  51.9 4.1 %collective-permute-start.5 = (f32[480,128]{1,0:T(8,128)S(1)}, f32[480,128]{1,0:T(8,128)S(1)}, u32[]{:S(2)}, u32[]{:S(2)}) collective-permute-start(f32[480,128]{1,0:T(8,128)S(1)} %slice_add_fusion.mine), channel_id=1, source_target_pairs={{0,2},{2,0},{4,6},{6,4},{1,3},{3,1},{5,7},{7,5},{8,10},{10,8},{12,... | collective-permute-start | bytes 737288 | tf_op jit(solution)/shard_map/ppermute | solution.py:556
  52.1 0.9 %copy-start.1 = (f32[64,128]{1,0:T(8,128)S(1)}, f32[64,128]{1,0:T(8,128)}, u32[]{:S(2)}) copy-start(f32[64,128]{1,0:T(8,128)} %get-tuple-element.16.eddy) | copy-start | bytes 98308
  52.1 0.8 %copy-start.2 = (s32[8]{0:T(128)S(1)}, s32[8]{0:T(128)}, u32[]{:S(2)}) copy-start(s32[8]{0:T(128)} %stack.23) | copy-start | bytes 100
  52.9 3.1 %copy-start.3 = (s32[1,1,32,1]{2,3,1,0:T(1,128)S(1)}, s32[1,1,32,1]{2,3,1,0:T(1,128)}, u32[]{:S(2)}) copy-start(s32[1,1,32,1]{2,3,1,0:T(1,128)} %param.12) | copy-start | bytes 388
  52.9 3.1 %copy-start.4 = (s32[1,1,32,1]{2,3,1,0:T(1,128)S(1)}, s32[1,1,32,1]{2,3,1,0:T(1,128)}, u32[]{:S(2)}) copy-start(s32[1,1,32,1]{2,3,1,0:T(1,128)} %param.13) | copy-start | bytes 388

commit v3 on v2

--- a/solution.py
+++ b/solution.py
@@ -44,18 +44,20 @@
     return lax.dot_general(a, b, (((1,), (0,)), ((), ())), preferred_element_type=F32, precision=precision)
 
 
+def core_half(at):
+    return (at ^ (at >> 1)) & 1
+
+
 def net_kernel(
-    scal, vel, tgt, w1, w2, w3, own, blk,
+    vel, tgt, w1, w2, w3, own, blk,
     keep, send, eddy_out, halo1, halo2, halo3, halo4,
     hx_a, hx_b, hy_b, hz, pool_s, fp_s, i1_s, a_s, d_s, tt_s, tb_s, pre_s, slope1_s, ah_s, slope2_s, dw_s, big_s, gh_s,
 ):
-    trainers = scal[0, 0]
-    gx_at = scal[0, 1]
-    gy_at = scal[0, 2]
-    half = scal[0, 3]
-    dev = scal[0, 4]
-    gx_odd = gx_at % 2 == 1
-    gy_odd = gy_at % 2 == 1
+    gx_at, gy_at = lax.axis_index("gx"), lax.axis_index("gy")
+    half = core_half(gy_at)
+    dev = (gx_at * lax.axis_size("gy") + gy_at) * lax.axis_size("role") + lax.axis_index("role")
+    trainers = lax.axis_size("gx") * lax.axis_size("gy") * lax.axis_size("role")
+    gx_odd, gy_odd = gx_at & 1 == 1, gy_at & 1 == 1
 
     for c in range(3):
         for x in range(SIDE):
@@ -157,7 +159,7 @@
     eddy = 0.5 * (jnp.maximum(logits, 0.0) + jnp.log1p(jnp.exp(-jnp.abs(logits))))
     error = eddy - target
     losses = jnp.sum(jnp.sum((error * error).reshape(64, BLK, SIDE), axis=0), axis=1, keepdims=True) / CELLS
-    d_logit = (error * jax.nn.sigmoid(logits) / (trainers.astype(F32) * CELLS)).astype(BF16)
+    d_logit = (error * jax.nn.sigmoid(logits) / (trainers * CELLS)).astype(BF16)
 
     zrep = onehot(iota((SIDE, 1), 0) == (iota((1, 128), 1) & 15) >> 1, F32)
     fine = nn(eddy, zrep, HIGH)
@@ -217,7 +219,10 @@
     low_half = iota((64, 128), 1) < 64
     for k in range(9):
         dx, j = k // 3, k % 3
-        big_s[:, 0:512] = nn(dwt, a_s[dx * SLAB : dx * SLAB + ROWS, j * 512 : (j + 1) * 512])
+        for q in range(2):
+            zs = slice(q * 192, q * 192 + 320)
+            cols = slice(j * 512 + q * 256, j * 512 + (q + 1) * 256)
+            big_s[zs, q * 256 : (q + 1) * 256] = nn(dwt[zs], a_s[dx * SLAB : dx * SLAB + ROWS, cols])
         sums = []
         for m in (-1, 0, 1, 2):
             tot = None
@@ -274,11 +279,11 @@
     g_last = jnp.sum(nt(fold_o, gl, HIGH), axis=1, keepdims=True)
 
     lane8 = iota((BLK, 128), 1)
-    loss_row = jnp.where(lane8 - (LOSS_COL + BLK * (dev // 64)) == iota((BLK, 128), 0), losses, 0.0)
+    loss_row = jnp.where(lane8 - (LOSS_COL + BLK * (dev >> 6)) == iota((BLK, 128), 0), losses, 0.0)
     loss_row = jnp.sum(loss_row, axis=0, keepdims=True)
     lane = iota((64, 128), 1)
     extra = jnp.where(lane == LAST_COL, g_last, g_first)
-    extra = extra + jnp.where(iota((64, 128), 0) == dev % 64, loss_row, 0.0)
+    extra = extra + jnp.where(iota((64, 128), 0) == dev & 63, loss_row, 0.0)
 
     for t in range(PAY // 128):
         if t == 0:
@@ -293,12 +298,12 @@
     return pl.BlockSpec(memory_space=pltpu.VMEM)
 
 
-def run_net(scal, velocity, target, w1, w2, w3, own, blk):
+def run_net(velocity, target, w1, w2, w3, own, blk):
     f = lambda *s: jax.ShapeDtypeStruct(s, F32)
     return pl.pallas_call(
         net_kernel,
         out_shape=(f(480, 128), f(584, 128), f(64, 128)) + (f(104, 128),) * 4,
-        in_specs=[pl.BlockSpec(memory_space=pltpu.SMEM)] + [vmem_spec()] * 7,
+        in_specs=[vmem_spec()] * 7,
         out_specs=tuple(vmem_spec() for _ in range(7)),
         scratch_shapes=[
             pltpu.VMEM((104, 128), F32),
@@ -322,15 +327,15 @@
         ],
         compiler_params=pltpu.CompilerParams(vmem_limit_bytes=56 * 1024 * 1024),
         name="net",
-    )(scal, velocity, target, w1, w2, w3, own, blk)
+    )(velocity, target, w1, w2, w3, own, blk)
 
 
 def flow_kernel(
-    scal, vel, eddy, got0, got1, got2, got3, got4, out, rx_a, rx_b, ry_a, ry_b, rz, vx_s, vy_s, visc_s, ez_s
+    vel, eddy, got0, got1, got2, got3, got4, out, rx_a, rx_b, ry_a, ry_b, rz, vx_s, vy_s, visc_s, ez_s
 ):
-    gx_odd = scal[0, 1] % 2 == 1
-    gy_odd = scal[0, 2] % 2 == 1
-    second = scal[0, 3] == 1
+    gx_at, gy_at = lax.axis_index("gx"), lax.axis_index("gy")
+    gx_odd, gy_odd = gx_at & 1 == 1, gy_at & 1 == 1
+    second = core_half(gy_at) == 1
     ry_a[...] = got0[...]
     ry_b[...] = jnp.where(second, got2[...], got1[...])
     rx_a[...] = jnp.where(second, got1[...], got3[...])
@@ -425,11 +430,11 @@
             out[c, x] = u + time_step * (diffuse - advect)
 
 
-def run_flow(scal, velocity, eddy, *got):
+def run_flow(velocity, eddy, *got):
     return pl.pallas_call(
         flow_kernel,
         out_shape=jax.ShapeDtypeStruct(velocity.shape, F32),
-        in_specs=[pl.BlockSpec(memory_space=pltpu.SMEM)] + [vmem_spec()] * 7,
+        in_specs=[vmem_spec()] * 7,
         out_specs=vmem_spec(),
         scratch_shapes=[
             pltpu.VMEM((104, 128), F32),
@@ -444,11 +449,14 @@
         ],
         compiler_params=pltpu.CompilerParams(vmem_limit_bytes=32 * 1024 * 1024),
         name="flow",
-    )(scal, velocity, eddy, *got)
-
-
-def finish_kernel(scal, own, blk, mine, other, loss_out, first_out, hidden_out, last_out, ext_s):
-    second = scal[0, 3] == 1
+    )(velocity, eddy, *got)
+
+
+def finish_kernel(own, blk, mine, other, loss_out, first_out, hidden_out, last_out, ext_s):
+    gx_at, gy_at = lax.axis_index("gx"), lax.axis_index("gy")
+    n_z = lax.axis_size("role")
+    in_group = gy_at * n_z + lax.axis_index("role")
+    second = core_half(gy_at) == 1
     for t in range(PAY // 128):
         one, two = mine[t * 32 : (t + 1) * 32, :], other[t * 32 : (t + 1) * 32, :]
         top, bottom = jnp.where(second, two, one), jnp.where(second, one, two)
@@ -469,38 +477,32 @@
     slot_lane = iota((1, slots), 1)
     picked = jnp.zeros((1, slots), F32)
     for s in range(slots):
-        at = scal[0, 1] * slots + s
-        dev = own[0, at] * scal[0, 5] + scal[0, 6]
-        row = ext_s[pl.ds(dev % 64, 1), :]
-        col = LOSS_COL + BLK * (dev // 64) + blk[0, at]
+        at = gx_at * slots + s
+        dev = own[0, at] * (lax.axis_size("gy") * n_z) + in_group
+        row = ext_s[pl.ds(dev & 63, 1), :]
+        col = LOSS_COL + BLK * (dev >> 6) + blk[0, at]
         value = jnp.sum(jnp.where(lane == col, row, 0.0), axis=1, keepdims=True)
         picked = jnp.where(slot_lane == s, value, picked)
     loss_out[...] = picked
 
 
-def run_finish(scal, own, blk, mine, other, slots):
+def run_finish(own, blk, mine, other, slots):
     smem = pl.BlockSpec(memory_space=pltpu.SMEM)
     f = lambda *s: jax.ShapeDtypeStruct(s, F32)
     return pl.pallas_call(
         finish_kernel,
         out_shape=(f(1, slots), f(64, 81), f(64, 27 * CH), f(1, 64)),
-        in_specs=[smem] * 3 + [vmem_spec()] * 2,
+        in_specs=[smem] * 2 + [vmem_spec()] * 2,
         out_specs=tuple(vmem_spec() for _ in range(4)),
         scratch_shapes=[pltpu.VMEM((64, 128), F32)],
         compiler_params=pltpu.CompilerParams(vmem_limit_bytes=32 * 1024 * 1024),
         name="finish",
-    )(scal, own, blk, mine, other)
+    )(own, blk, mine, other)
 
 
 def on_device(velocity, target_visc, w_first, w_hidden, w_last, sample_owner, sample_block):
     n_x, n_y, n_z = lax.axis_size("gx"), lax.axis_size("gy"), lax.axis_size("role")
     trainers = n_x * n_y * n_z
-    at_x, at_y, at_z = lax.axis_index("gx"), lax.axis_index("gy"), lax.axis_index("role")
-    group = at_y * n_z + at_z
-    half = (at_y ^ (at_y >> 1)) & 1
-    scal = jnp.stack(
-        [jnp.int32(trainers), at_x, at_y, half, at_x * (n_y * n_z) + group, jnp.int32(n_y * n_z), group, jnp.int32(0)]
-    ).astype(jnp.int32)[None]
     own = sample_owner.reshape(1, -1)
     blk = sample_block.reshape(1, -1)
     slots = own.shape[1] // n_x
@@ -536,27 +538,38 @@
     size = PAY // 4
 
     keep, send, eddy, *halos = run_net(
-        scal, velocity, target_visc, w_first, w_hidden, w_last.reshape(1, CH), own, blk
+        velocity, target_visc, w_first, w_hidden, w_last.reshape(1, CH), own, blk
     )
+    half = core_half(lax.axis_index("gy"))
     got = lax.ppermute(send, "gy", core_pairs)
     total = keep + got[:size]
     rims = [got[size:]]
     orders = (("x", "y", "z_a", "z_b"), ("z_a", "x", "z_b", "y"))
+    far = None
     for s in range(4):
         kinds = (orders[0][s], orders[1][s])
-        got = lax.ppermute(jnp.concatenate([total, halos[s]], axis=0), axes, mixed(kinds))
+        if s == 1:
+            far = lax.ppermute(halos[3], axes, mixed((orders[0][3], orders[1][3])))
+        if s < 3:
+            got = lax.ppermute(jnp.concatenate([total, halos[s]], axis=0), axes, mixed(kinds))
+            rims.append(got[size:])
+        else:
+            got = lax.ppermute(total, axes, mixed(kinds))
         part = got[:size]
         if n_x != 4 and "z_b" in kinds:
             part = jnp.where(half == kinds.index("z_b"), 0.0, part)
         total = total + part
-        rims.append(got[size:])
+        if s == 1:
+            total, far = lax.optimization_barrier((total, far))
+        if s == 2:
+            u_next = run_flow(velocity, eddy, *rims, far)
+    total, u_next = lax.optimization_barrier((total, u_next))
     if n_x != 4:
         for bit in range(1, n_x.bit_length() - 1):
             total = total + lax.ppermute(total, "gx", [(i, i ^ (1 << bit)) for i in range(n_x)])
     other = lax.ppermute(total, "gy", core_pairs)
 
-    u_next = run_flow(scal, velocity, eddy, *rims)
-    losses, first, hidden, last = run_finish(scal, own, blk, total, other, slots)
+    losses, first, hidden, last = run_finish(own, blk, total, other, slots)
     return (u_next, losses.reshape(1, 1, slots), first, hidden, last.reshape(CH))
 
 

time: 58.5 us -> 53.8 us (0.920); the launches traced: 57.5 us -> 53.6 us
  waiting for transfers between devices: 22.9 us -> 19.3 us
  starting transfers between devices: 12.1 us -> 14.2 us
  Pallas kernels: 19 us -> 17.4 us
  local copies, waits for them, and re-layouts: 1.48 us -> 0.78 us
    ppermute x0 -> x2, starting transfers between devices: none -> 7.28 us  [the longest x1 3.67 us: on_device(): got = lax.ppermute(total, axes, mixed(kinds))]
    ppermute x4 -> x3, waiting for transfers between devices: 21.5 us -> 14.6 us  [on_device(): lax.ppermute(jnp.concatenate([total, halos[s]], axis=0), axes, mixed(kinds))]
    ppermute x4 -> x3, starting transfers between devices: 11.6 us -> 6.33 us  [on_device(): lax.ppermute(jnp.concatenate([total, halos[s]], axis=0), axes, mixed(kinds))]
    ppermute x0 -> x2, waiting for transfers between devices: none -> 1.78 us  [the longest x1 1.2 us: on_device(): got = lax.ppermute(total, axes, mixed(kinds))]
    ppermute x1, waiting for transfers between devices: 0.01 us -> 1.5 us  [on_device(): other = lax.ppermute(total, 'gy', core_pairs)]
    pallas_call x1, Pallas kernels: 14.5 us -> 13.5 us  [run_net(): pl.pallas_call(net_kernel, out_shape=(f(480, 128), f(584, 128), f(64, 128...]
    pallas_call x1, Pallas kernels: 3.13 us -> 2.5 us  [run_flow(): pl.pallas_call(flow_kernel, out_shape=jax.ShapeDtypeStruct(velocity.shape...]
    another operation x1 -> x0, local copies, waits for them, and re-layouts: 0.6 us -> none  [on_device(): jnp.stack([jnp.int32(trainers), at_x, at_y, half, at_x * (n_y * n_z) + gr...]
  transfers between devices with their start and end apart: 6 -> 7, of which waited for: 5 -> 7; matrix products, arithmetic and copies ran while one was open for 0% -> 0% of each run, Pallas kernels for 5% -> 5%
where the time goes in v3:
time: 53.8 us; the launch traced here: 53.6 us
  waiting for transfers between devices  19.3 us (36%)
  Pallas kernels  17.4 us (32%)
  starting transfers between devices  14.2 us (26%)
  other arithmetic  1.17 us (2%)
  local copies, waits for them, and re-layouts  0.78 us (1%)
  between operations  0.76 us (1%)
    ppermute x3, waiting for transfers between devices, on_device(): lax.ppermute(jnp.concatenate([total, halos[s]], axis=0), axes, mixed(kinds))  14.6 us
    pallas_call x1, Pallas kernels, run_net(): pl.pallas_call(net_kernel, out_shape=(f(480, 128), f(584, 128), f(64, 128...  13.5 us
    ppermute x3, starting transfers between devices, on_device(): lax.ppermute(jnp.concatenate([total, halos[s]], axis=0), axes, mixed(kinds))  6.33 us
    ppermute x1, starting transfers between devices, on_device(): got = lax.ppermute(total, axes, mixed(kinds))  3.67 us
    ppermute x1, starting transfers between devices, on_device(): far = lax.ppermute(halos[3], axes, mixed((orders[0][3], orders[1][3])))  3.61 us
    pallas_call x1, Pallas kernels, run_flow(): pl.pallas_call(flow_kernel, out_shape=jax.ShapeDtypeStruct(velocity.shape...  2.5 us
    ppermute x1, waiting for transfers between devices, on_device(): other = lax.ppermute(total, 'gy', core_pairs)  1.5 us
    ppermute x1, waiting for transfers between devices, on_device(): got = lax.ppermute(send, 'gy', core_pairs)  1.43 us
  transfers between devices with their start and end apart: 7, of which 7 were waited for; matrix products, arithmetic and copies ran while one was open for 0% of the time, Pallas kernels for 5%

profile of v3, /device:TPU:0, one launch (start us, length us, event | category | flops | bytes accessed | tf_op | source)
XLA Modules:
  0.0 53.6 jit_solution(18045665176120201764)
XLA Ops:
  0.6 13.5 %net.1 = (f32[480,128]{1,0:T(8,128)}, f32[584,128]{1,0:T(8,128)}, f32[64,128]{1,0:T(8,128)}, f32[104,128]{1,0:T(8,128)}, f32[104,128]{1,0:T(8,128)}, /*index=5*/f32[104,128]{1,0:T(8,128)}, f32[104,128]{1,0:T(8,128)}) custom-call(f32[3,16,16,128]{3,2,1,0:T(8,128)} %vel.3, bf16[8,8,64]{2,1,0:T(8,128)(2,1)} %tgt.1, bf16[64,81]{1,0:T(8,128)(2,1)} %w1.1, ...), custom_call_target="tpu_custom_call" | custom-call | tf_op jit(solution)/shard_map/net/pallas_call | solution.py:303
  14.2 0.5 collective-permute-start
  14.6 1.4 %collective-permute-done = f32[584,128]{1,0:T(8,128)S(1)} collective-permute-done((f32[584,128]{1,0:T(8,128)}, f32[584,128]{1,0:T(8,128)S(1)}, u32[]{:S(2)}, u32[]{:S(2)}) %collective-permute-start) | collective-permute-done | bytes 299040 | tf_op jit(solution)/shard_map/ppermute | solution.py:544
  16.0 1.0 %slice_add_fusion.3 = f32[480,128]{1,0:T(8,128)S(1)} fusion(f32[480,128]{1,0:T(8,128)} %get-tuple-element.20, f32[584,128]{1,0:T(8,128)S(1)} %collective-permute-done), kind=kLoop, calls=%fused_computation.6 | loop fusion | flops 61440 | bytes 737280 | tf_op jit(solution)/shard_map/add | solution.py:545
  17.0 0.0 copy-done.6
  17.1 2.7 %collective-permute-start.1 = (f32[584,128]{1,0:T(8,128)S(1)}, f32[584,128]{1,0:T(8,128)S(1)}, u32[]{:S(2)}, u32[]{:S(2)}) collective-permute-start(f32[584,128]{1,0:T(8,128)S(1)} %pad_maximum_fusion), channel_id=1, source_target_pairs={{0,6},{1,7},{2,10},{3,11},{4,12},{5,13},{6,0},{7,1},{8,14},{9,15},... | collective-permute-start | bytes 897032 | tf_op jit(solution)/shard_map/ppermute | solution.py:554
  19.7 4.5 %collective-permute-done.1 = f32[584,128]{1,0:T(8,128)S(1)} collective-permute-done((f32[584,128]{1,0:T(8,128)S(1)}, f32[584,128]{1,0:T(8,128)S(1)}, u32[]{:S(2)}, u32[]{:S(2)}) %collective-permute-start.1) | collective-permute-done | bytes 299040 | tf_op jit(solution)/shard_map/ppermute | solution.py:554
  24.2 0.0 copy-done.5
  24.2 0.0 copy-start.7
  24.3 2.1 %collective-permute-start.2 = (f32[584,128]{1,0:T(8,128)S(1)}, f32[584,128]{1,0:T(8,128)S(1)}, u32[]{:S(2)}, u32[]{:S(2)}) collective-permute-start(f32[584,128]{1,0:T(8,128)S(1)} %pad_maximum_fusion.1), channel_id=1, source_target_pairs={{0,1},{1,0},{2,4},{3,5},{4,2},{5,3},{6,7},{7,6},{8,9},{9,8},{10,12... | collective-permute-start | bytes 897032 | tf_op jit(solution)/shard_map/ppermute | solution.py:554
  26.4 3.6 %collective-permute-start.3 = (f32[104,128]{1,0:T(8,128)S(1)}, f32[104,128]{1,0:T(8,128)S(1)}, u32[]{:S(2)}, u32[]{:S(2)}) collective-permute-start(f32[104,128]{1,0:T(8,128)S(1)} %copy-done.7), channel_id=1, source_target_pairs={{0,24},{1,25},{2,3},{3,2},{4,5},{5,4},{6,30},{7,31},{8,16},{9,17},... | collective-permute-start | bytes 159752 | tf_op jit(solution)/shard_map/ppermute | solution.py:552
  30.0 1.7 %collective-permute-done.2 = f32[584,128]{1,0:T(8,128)S(1)} collective-permute-done((f32[584,128]{1,0:T(8,128)S(1)}, f32[584,128]{1,0:T(8,128)S(1)}, u32[]{:S(2)}, u32[]{:S(2)}) %collective-permute-start.2) | collective-permute-done | bytes 299040 | tf_op jit(solution)/shard_map/ppermute | solution.py:554
  31.7 0.6 %collective-permute-done.3.got4 = f32[104,128]{1,0:T(8,128)S(1)} collective-permute-done((f32[104,128]{1,0:T(8,128)S(1)}, f32[104,128]{1,0:T(8,128)S(1)}, u32[]{:S(2)}, u32[]{:S(2)}) %collective-permute-start.3) | collective-permute-done | bytes 53280 | tf_op jit(solution)/shard_map/ppermute | solution.py:552
  32.3 1.6 %collective-permute-start.4 = (f32[584,128]{1,0:T(8,128)S(1)}, f32[584,128]{1,0:T(8,128)S(1)}, u32[]{:S(2)}, u32[]{:S(2)}) collective-permute-start(f32[584,128]{1,0:T(8,128)S(1)} %pad_maximum_fusion.2), channel_id=1, source_target_pairs={{0,8},{1,9},{2,26},{3,27},{4,28},{5,29},{6,14},{7,15},{8,0},{9,1},... | collective-permute-start | bytes 897032 | tf_op jit(solution)/shard_map/ppermute | solution.py:554
  33.9 8.5 %collective-permute-done.4 = f32[584,128]{1,0:T(8,128)S(1)} collective-permute-done((f32[584,128]{1,0:T(8,128)S(1)}, f32[584,128]{1,0:T(8,128)S(1)}, u32[]{:S(2)}, u32[]{:S(2)}) %collective-permute-start.4) | collective-permute-done | bytes 299040 | tf_op jit(solution)/shard_map/ppermute | solution.py:554
  42.4 0.0 copy-start
  42.4 3.7 %collective-permute-start.5 = (f32[480,128]{1,0:T(8,128)S(1)}, f32[480,128]{1,0:T(8,128)S(1)}, u32[]{:S(2)}, u32[]{:S(2)}) collective-permute-start(f32[480,128]{1,0:T(8,128)S(1)} %slice_add_fusion), channel_id=1, source_target_pairs={{0,24},{1,25},{2,3},{3,2},{4,5},{5,4},{6,30},{7,31},{8,16},{9,17},... | collective-permute-start | bytes 737288 | tf_op jit(solution)/shard_map/ppermute | solution.py:557
  46.1 0.0 copy-start.1
  46.2 0.7 %copy-done.1 = f32[64,128]{1,0:T(8,128)S(1)} copy-done((f32[64,128]{1,0:T(8,128)S(1)}, f32[64,128]{1,0:T(8,128)}, u32[]{:S(2)}) %copy-start.1) | copy-done | bytes 32792
  46.9 2.5 %flow.1 = f32[3,16,16,128]{3,2,1,0:T(8,128)} custom-call(f32[3,16,16,128]{3,2,1,0:T(8,128)S(1)} %copy-done, f32[64,128]{1,0:T(8,128)S(1)} %copy-done.1, f32[104,128]{1,0:T(8,128)S(1)} %slice.36.got0, f32[104,128]{1,0:T(8,128)S(1)} %slice.37.got1, f32[104,128]{1,0:T(8,128)S(1)} %slice.38.got2, f32[104,128]{1,0:T(8,128)S(1)} %slice.39.got3, ...), custom_call_target="tpu_custom_call" | custom-call | tf_op jit(solution)/shard_map/flow/pallas_call | solution.py:434
  49.4 1.2 %collective-permute-done.5 = f32[480,128]{1,0:T(8,128)S(1)} collective-permute-done((f32[480,128]{1,0:T(8,128)S(1)}, f32[480,128]{1,0:T(8,128)S(1)}, u32[]{:S(2)}, u32[]{:S(2)}) %collective-permute-start.5) | collective-permute-done | bytes 245792 | tf_op jit(solution)/shard_map/ppermute | solution.py:557
  50.6 0.1 collective-permute-start.6
  50.7 1.5 %collective-permute-done.6.other = f32[480,128]{1,0:T(8,128)S(1)} collective-permute-done((f32[480,128]{1,0:T(8,128)S(1)}, f32[480,128]{1,0:T(8,128)S(1)}, u32[]{:S(2)}, u32[]{:S(2)}) %collective-permute-start.6) | collective-permute-done | bytes 245792 | tf_op jit(solution)/shard_map/ppermute | solution.py:570
  52.2 1.4 %finish.1 = (f32[1,8]{1,0:T(1,128)}, f32[64,81]{1,0:T(8,128)}, f32[64,1728]{1,0:T(8,128)}, f32[1,64]{1,0:T(1,128)}) custom-call(s32[1,32]{1,0:T(1,128)S(1)} %bitcast.6, s32[1,32]{1,0:T(1,128)S(1)} %bitcast.8, f32[480,128]{1,0:T(8,128)S(1)} %add.19.mine, f32[480,128]{1,0:T(8,128)S(1)} %collective-permute-done.6.other), custom_call_target="tpu_custom_call" | custom-call | tf_op jit(solution)/shard_map/finish/pallas_call | solution.py:492
  (21 shorter events, 0.2 us)
Async XLA Ops:
  14.2 1.9 %collective-permute-start = (f32[584,128]{1,0:T(8,128)}, f32[584,128]{1,0:T(8,128)S(1)}, u32[]{:S(2)}, u32[]{:S(2)}) collective-permute-start(f32[584,128]{1,0:T(8,128)} %get-tuple-element.21), channel_id=1, source_target_pairs={{0,2},{2,0},{4,6},{6,4},{1,3},{3,1},{5,7},{7,5},{8,10},{10,8},{12,... | collective-permute-start | bytes 897032 | tf_op jit(solution)/shard_map/ppermute | solution.py:544
  16.0 1.0 %copy-start.6 = (f32[104,128]{1,0:T(8,128)S(1)}, f32[104,128]{1,0:T(8,128)}, u32[]{:S(2)}) copy-start(f32[104,128]{1,0:T(8,128)} %get-tuple-element.22) | copy-start | bytes 159748
  17.1 7.2 %copy-start.5 = (f32[104,128]{1,0:T(8,128)S(1)}, f32[104,128]{1,0:T(8,128)}, u32[]{:S(2)}) copy-start(f32[104,128]{1,0:T(8,128)} %get-tuple-element.23) | copy-start | bytes 159748
  17.1 7.1 %collective-permute-start.1 = (f32[584,128]{1,0:T(8,128)S(1)}, f32[584,128]{1,0:T(8,128)S(1)}, u32[]{:S(2)}, u32[]{:S(2)}) collective-permute-start(f32[584,128]{1,0:T(8,128)S(1)} %pad_maximum_fusion), channel_id=1, source_target_pairs={{0,6},{1,7},{2,10},{3,11},{4,12},{5,13},{6,0},{7,1},{8,14},{9,15},... | collective-permute-start | bytes 897032 | tf_op jit(solution)/shard_map/ppermute | solution.py:554
  24.2 2.1 %copy-start.7 = (f32[104,128]{1,0:T(8,128)S(1)}, f32[104,128]{1,0:T(8,128)}, u32[]{:S(2)}) copy-start(f32[104,128]{1,0:T(8,128)} %get-tuple-element.24) | copy-start | bytes 159748
  24.3 7.4 %collective-permute-start.2 = (f32[584,128]{1,0:T(8,128)S(1)}, f32[584,128]{1,0:T(8,128)S(1)}, u32[]{:S(2)}, u32[]{:S(2)}) collective-permute-start(f32[584,128]{1,0:T(8,128)S(1)} %pad_maximum_fusion.1), channel_id=1, source_target_pairs={{0,1},{1,0},{2,4},{3,5},{4,2},{5,3},{6,7},{7,6},{8,9},{9,8},{10,12... | collective-permute-start | bytes 897032 | tf_op jit(solution)/shard_map/ppermute | solution.py:554
  26.4 5.9 %copy-start.4 = (f32[104,128]{1,0:T(8,128)S(1)}, f32[104,128]{1,0:T(8,128)}, u32[]{:S(2)}) copy-start(f32[104,128]{1,0:T(8,128)} %get-tuple-element.26) | copy-start | bytes 159748
  26.4 5.9 %collective-permute-start.3 = (f32[104,128]{1,0:T(8,128)S(1)}, f32[104,128]{1,0:T(8,128)S(1)}, u32[]{:S(2)}, u32[]{:S(2)}) collective-permute-start(f32[104,128]{1,0:T(8,128)S(1)} %copy-done.7), channel_id=1, source_target_pairs={{0,24},{1,25},{2,3},{3,2},{4,5},{5,4},{6,30},{7,31},{8,16},{9,17},... | collective-permute-start | bytes 159752 | tf_op jit(solution)/shard_map/ppermute | solution.py:552
  32.3 10.0 %collective-permute-start.4 = (f32[584,128]{1,0:T(8,128)S(1)}, f32[584,128]{1,0:T(8,128)S(1)}, u32[]{:S(2)}, u32[]{:S(2)}) collective-permute-start(f32[584,128]{1,0:T(8,128)S(1)} %pad_maximum_fusion.2), channel_id=1, source_target_pairs={{0,8},{1,9},{2,26},{3,27},{4,28},{5,29},{6,14},{7,15},{8,0},{9,1},... | collective-permute-start | bytes 897032 | tf_op jit(solution)/shard_map/ppermute | solution.py:554
  42.4 3.7 %copy-start = (f32[3,16,16,128]{3,2,1,0:T(8,128)S(1)}, f32[3,16,16,128]{3,2,1,0:T(8,128)}, u32[]{:S(2)}) copy-start(f32[3,16,16,128]{3,2,1,0:T(8,128)} %vel.3) | copy-start | bytes 1179652
  42.4 8.2 %collective-permute-start.5 = (f32[480,128]{1,0:T(8,128)S(1)}, f32[480,128]{1,0:T(8,128)S(1)}, u32[]{:S(2)}, u32[]{:S(2)}) collective-permute-start(f32[480,128]{1,0:T(8,128)S(1)} %slice_add_fusion), channel_id=1, source_target_pairs={{0,24},{1,25},{2,3},{3,2},{4,5},{5,4},{6,30},{7,31},{8,16},{9,17},... | collective-permute-start | bytes 737288 | tf_op jit(solution)/shard_map/ppermute | solution.py:557
  46.1 0.8 %copy-start.1 = (f32[64,128]{1,0:T(8,128)S(1)}, f32[64,128]{1,0:T(8,128)}, u32[]{:S(2)}) copy-start(f32[64,128]{1,0:T(8,128)} %get-tuple-element.27.eddy) | copy-start | bytes 98308
  49.4 2.8 %copy-start.2 = (s32[1,1,32,1]{2,3,1,0:T(1,128)S(1)}, s32[1,1,32,1]{2,3,1,0:T(1,128)}, u32[]{:S(2)}) copy-start(s32[1,1,32,1]{2,3,1,0:T(1,128)} %param.12) | copy-start | bytes 388
  49.4 2.8 %copy-start.3 = (s32[1,1,32,1]{2,3,1,0:T(1,128)S(1)}, s32[1,1,32,1]{2,3,1,0:T(1,128)}, u32[]{:S(2)}) copy-start(s32[1,1,32,1]{2,3,1,0:T(1,128)} %param.13) | copy-start | bytes 388
  50.6 1.6 %collective-permute-start.6 = (f32[480,128]{1,0:T(8,128)S(1)}, f32[480,128]{1,0:T(8,128)S(1)}, u32[]{:S(2)}, u32[]{:S(2)}) collective-permute-start(f32[480,128]{1,0:T(8,128)S(1)} %add.19.mine), channel_id=1, source_target_pairs={{0,2},{2,0},{4,6},{6,4},{1,3},{3,1},{5,7},{7,5},{8,10},{10,8},{12,... | collective-permute-start | bytes 737288 | tf_op jit(solution)/shard_map/ppermute | solution.py:570

commit v4 on v3

--- a/solution.py
+++ b/solution.py
@@ -16,9 +16,13 @@
 ROWS = SIDE * SIDE * BLK
 WIDE = SIDE * CH
 SLAB = SIDE * BLK
-PAY = 1920
+TILES = 15
+PAY = TILES * 128
 LAST_COL = 81
 LOSS_COL = 82
+
+EDDY_SCALE = 2.0**-9
+F16 = jnp.float16
 
 base_visc = 0.02
 time_step = 0.2
@@ -173,8 +177,9 @@
             at = (c * 2 + i) * 16
             hx_a[at : at + 16, :] = jnp.where(gx_odd, lo, hi)
             hx_b[at : at + 16, :] = jnp.where(gx_odd, hi, lo)
-    hx_a[96:104, :] = jnp.where(gx_odd, fine[0:8], fine[56:64])
-    hx_b[96:104, :] = jnp.where(gx_odd, fine[56:64], fine[0:8])
+    small = fine * EDDY_SCALE
+    hx_a[96:104, :] = jnp.where(gx_odd, small[0:8], small[56:64])
+    hx_b[96:104, :] = jnp.where(gx_odd, small[56:64], small[0:8])
     core = send.at[480:584]
     for c in range(3):
         for i in range(2):
@@ -183,12 +188,12 @@
             at = (c * 2 + i) * 16
             core[at : at + 16, :] = jnp.where(gy_odd, lo, hi)
             hy_b[at : at + 16, :] = jnp.where(gy_odd, hi, lo)
-    lo = eddy_out[pl.ds(0, 8, stride=8), :]
-    hi = eddy_out[pl.ds(7, 8, stride=8), :]
+    lo = eddy_out[pl.ds(0, 8, stride=8), :] * EDDY_SCALE
+    hi = eddy_out[pl.ds(7, 8, stride=8), :] * EDDY_SCALE
     core[96:104, :] = jnp.where(gy_odd, lo, hi)
     hy_b[96:104, :] = jnp.where(gy_odd, hi, lo)
     vt = jnp.transpose(vel[...].reshape(768, 128))
-    et = jnp.transpose(jnp.concatenate([fine, jnp.zeros((64, 128), F32)], axis=0))
+    et = jnp.transpose(jnp.concatenate([small, jnp.zeros((64, 128), F32)], axis=0))
     hz[...] = jnp.zeros(hz.shape, F32)
     for t in range(6):
         hz[t * 8 : t * 8 + 2, :] = vt[0:2, t * 128 : (t + 1) * 128]
@@ -299,7 +304,7 @@
 
 
 def run_net(velocity, target, w1, w2, w3, own, blk):
-    f = lambda *s: jax.ShapeDtypeStruct(s, F32)
+    f = lambda *s: pltpu.VMEM(s, F32)
     return pl.pallas_call(
         net_kernel,
         out_shape=(f(480, 128), f(584, 128), f(64, 128)) + (f(104, 128),) * 4,
@@ -360,11 +365,11 @@
 
     zcols = jnp.concatenate([jnp.transpose(rz[t * 8 : t * 8 + 8, :]) for t in range(7)], axis=0)
     coarse = eddy[...]
-    e_first, e_last = zcols[768:832, 0:1], zcols[768:832, 1:2]
+    e_first, e_last = zcols[768:832, 0:1] / EDDY_SCALE, zcols[768:832, 1:2] / EDDY_SCALE
     ahead = jnp.where(lane == 127, e_first, pltpu.roll(coarse, 127, 1))
     behind = jnp.where(lane == 0, e_last, pltpu.roll(coarse, 1, 1))
-    below_x, above_x = sides(gx_odd, rx_a, rx_b, 96, 8)
-    below_y, above_y = sides(gy_odd, ry_a, ry_b, 96, 8)
+    below_x, above_x = (v / EDDY_SCALE for v in sides(gx_odd, rx_a, rx_b, 96, 8))
+    below_y, above_y = (v / EDDY_SCALE for v in sides(gy_odd, ry_a, ry_b, 96, 8))
 
     def put(dst, plane, val):
         dst[pl.ds(plane * 32 + 8, 8, stride=2), :] = val
@@ -535,7 +540,7 @@
         return pairs
 
     core_pairs = [(j, even_odd(j, n_y)) for j in range(n_y)]
-    size = PAY // 4
+    size = TILES * 32
 
     keep, send, eddy, *halos = run_net(
         velocity, target_visc, w_first, w_hidden, w_last.reshape(1, CH), own, blk
@@ -544,25 +549,37 @@
     got = lax.ppermute(send, "gy", core_pairs)
     total = keep + got[:size]
     rims = [got[size:]]
+    halos = [h.astype(F16) for h in halos]
+
+    def widen(values, exps):
+        wide = values.astype(F32).reshape(TILES, 32, 128) * jnp.exp2(exps)[:, None, :]
+        return wide.reshape(size, 128)
+
+    top = jnp.max(jnp.abs(total.reshape(TILES, 32, 128)), axis=1)
+    exps = jnp.clip(jnp.ceil(jnp.log2(jnp.maximum(top, 1e-30))) - 13.0, -110.0, 110.0)
     orders = (("x", "y", "z_a", "z_b"), ("z_a", "x", "z_b", "y"))
     far = None
     for s in range(4):
         kinds = (orders[0][s], orders[1][s])
         if s == 1:
             far = lax.ppermute(halos[3], axes, mixed((orders[0][3], orders[1][3])))
+        scaled = total.reshape(TILES, 32, 128) * jnp.exp2(-exps)[:, None, :]
+        pieces = [scaled.reshape(size, 128).astype(F16), jnp.pad(exps, ((0, 1), (0, 0))).astype(F16)]
+        message = jnp.concatenate(pieces + [halos[s]] if s < 3 else pieces, axis=0)
+        message = lax.optimization_barrier(message)
+        got = lax.ppermute(message, axes, mixed(kinds))
+        their_exps = got[size : size + TILES].astype(F32)
+        mine, theirs = widen(message[:size], exps), widen(got[:size], their_exps)
+        if n_x != 4 and "z_b" in kinds:
+            theirs = jnp.where(half == kinds.index("z_b"), 0.0, theirs)
+        total = mine + theirs
+        exps = jnp.maximum(exps, their_exps) + 1.0
         if s < 3:
-            got = lax.ppermute(jnp.concatenate([total, halos[s]], axis=0), axes, mixed(kinds))
-            rims.append(got[size:])
-        else:
-            got = lax.ppermute(total, axes, mixed(kinds))
-        part = got[:size]
-        if n_x != 4 and "z_b" in kinds:
-            part = jnp.where(half == kinds.index("z_b"), 0.0, part)
-        total = total + part
+            rims.append(got[size + 16 :].astype(F32))
         if s == 1:
             total, far = lax.optimization_barrier((total, far))
         if s == 2:
-            u_next = run_flow(velocity, eddy, *rims, far)
+            u_next = run_flow(velocity, eddy, *rims, far.astype(F32))
     total, u_next = lax.optimization_barrier((total, u_next))
     if n_x != 4:
         for bit in range(1, n_x.bit_length() - 1):

time: 53.8 us -> 44.4 us (0.83)
  waiting for transfers between devices: 19.3 us -> 12.9 us
  starting transfers between devices: 14.2 us -> 13.2 us
  Pallas kernels: 17.4 us -> 16.6 us
  local copies, waits for them, and re-layouts: 0.78 us -> 0.02 us
    ppermute x4, waiting for transfers between devices: 15.8 us -> 10.2 us  [on_device(): got = lax.ppermute(message, axes, mixed(kinds))]
    ppermute x4, starting transfers between devices: 10 us -> 8.93 us  [on_device(): got = lax.ppermute(message, axes, mixed(kinds))]
    add x5 -> x2, other arithmetic: 1.11 us -> 0.1 us  [on_device(): total = mine + theirs]
    pallas_call x1, Pallas kernels: 13.5 us -> 12.7 us  [run_net(): pl.pallas_call(net_kernel, out_shape=(f(480, 128), f(584, 128), f(64, 128...]
    unnamed x16 -> x6, local copies, waits for them, and re-layouts: 0.76 us -> 0.01 us
    ppermute x1, waiting for transfers between devices: 0.58 us -> 0.01 us  [on_device(): far = lax.ppermute(halos[3], axes, mixed((orders[0][3], orders[1][3])))]
  transfers between devices with their start and end apart: 7 -> 7, of which waited for: 7 -> 5; matrix products, arithmetic and copies ran while one was open for 0% -> 1% of each run, Pallas kernels for 5% -> 6%
where the time goes in v4:
time: 44.4 us; the launch traced here: 44.2 us
  Pallas kernels  16.6 us (37%)
  starting transfers between devices  13.2 us (30%)
  waiting for transfers between devices  12.9 us (29%)
  between operations  0.81 us (2%)
  other arithmetic  0.71 us (2%)
    pallas_call x1, Pallas kernels, run_net(): pl.pallas_call(net_kernel, out_shape=(f(480, 128), f(584, 128), f(64, 128...  12.7 us
    ppermute x4, waiting for transfers between devices, on_device(): got = lax.ppermute(message, axes, mixed(kinds))  10.2 us
    ppermute x4, starting transfers between devices, on_device(): got = lax.ppermute(message, axes, mixed(kinds))  8.93 us
    ppermute x1, starting transfers between devices, on_device(): far = lax.ppermute(halos[3], axes, mixed((orders[0][3], orders[1][3])))  3.67 us
    pallas_call x1, Pallas kernels, run_flow(): pl.pallas_call(flow_kernel, out_shape=jax.ShapeDtypeStruct(velocity.shape...  2.5 us
    ppermute x1, waiting for transfers between devices, on_device(): other = lax.ppermute(total, 'gy', core_pairs)  1.5 us
    pallas_call x1, Pallas kernels, run_finish(): pl.pallas_call(finish_kernel, out_shape=(f(1, slots), f(64, 81), f(64, 27...  1.4 us
    ppermute x1, waiting for transfers between devices, on_device(): got = lax.ppermute(send, 'gy', core_pairs)  1.21 us
  transfers between devices with their start and end apart: 7, of which 5 were waited for; matrix products, arithmetic and copies ran while one was open for 1% of the time, Pallas kernels for 6%

profile of v4, /device:TPU:0, one launch (start us, length us, event | category | flops | bytes accessed | tf_op | source)
XLA Modules:
  0.0 44.2 jit_solution(3696768311571769538)
XLA Ops:
  0.6 12.7 %net.1 = (f32[480,128]{1,0:T(8,128)S(1)}, f32[584,128]{1,0:T(8,128)S(1)}, f32[64,128]{1,0:T(8,128)S(1)}, f32[104,128]{1,0:T(8,128)S(1)}, f32[104,128]{1,0:T(8,12...) custom-call(f32[3,16,16,128]{3,2,1,0:T(8,128)} %vel.3, bf16[8,8,64]{2,1,0:T(8,128)(2,1)} %tgt.1, ...), custom_call_target="tpu_custom_call" | custom-call | tf_op jit(solution)/shard_map/net/pallas_call | solution.py:308
  13.4 0.5 %collective-permute-start = (f32[584,128]{1,0:T(8,128)S(1)}, f32[584,128]{1,0:T(8,128)S(1)}, u32[]{:S(2)}, u32[]{:S(2)}) collective-permute-start(f32[584,128]{1,0:T(8,128)S(1)} %get-tuple-element.21), channel_id=1, source_target_pairs={{0,2},{2,0},{4,6},{6,4},{1,3},{3,1},{5,7},{7,5},{8,10},{10,8},{12,... | collective-permute-start | bytes 897032 | tf_op jit(solution)/shard_map/ppermute | solution.py:549
  13.9 1.2 %collective-permute-done = f32[584,128]{1,0:T(8,128)S(1)} collective-permute-done((f32[584,128]{1,0:T(8,128)S(1)}, f32[584,128]{1,0:T(8,128)S(1)}, u32[]{:S(2)}, u32[]{:S(2)}) %collective-permute-start) | collective-permute-done | bytes 299040 | tf_op jit(solution)/shard_map/ppermute | solution.py:549
  15.2 0.1 fusion.9
  15.3 2.7 %collective-permute-start.1 = (f16[600,128]{1,0:T(8,128)(2,1)S(1)}, f16[600,128]{1,0:T(8,128)(2,1)S(1)}, u32[]{:S(2)}, u32[]{:S(2)}) collective-permute-start(f16[600,128]{1,0:T(8,128)(2,1)S(1)} %fusion.14), channel_id=1, source_target_pairs={{0,6},{1,7},{2,10},{3,11},{4,12},{5,13},{6,0},{7,1},{8,14},{9,15},... | collective-permute-start | bytes 460808 | tf_op jit(solution)/shard_map/ppermute | solution.py:570
  18.0 3.7 %collective-permute-start.3 = (f16[104,128]{1,0:T(8,128)(2,1)S(1)}, f16[104,128]{1,0:T(8,128)(2,1)S(1)}, u32[]{:S(2)}, u32[]{:S(2)}) collective-permute-start(f16[104,128]{1,0:T(8,128)(2,1)S(1)} %convert_element_type.91), channel_id=1, source_target_pairs={{0,24},{1,25},{2,3},{3,2},{4,5},{5,4},{6,30},{7,31},{8,16},{9,17},... | collective-permute-start | bytes 79880 | tf_op jit(solution)/shard_map/ppermute | solution.py:565
  21.7 0.0 collective-permute-done.1
  21.7 0.1 fusion.7
  21.9 1.6 %collective-permute-start.2 = (f16[600,128]{1,0:T(8,128)(2,1)S(1)}, f16[600,128]{1,0:T(8,128)(2,1)S(1)}, u32[]{:S(2)}, u32[]{:S(2)}) collective-permute-start(f16[600,128]{1,0:T(8,128)(2,1)S(1)} %fusion.16), channel_id=1, source_target_pairs={{0,1},{1,0},{2,4},{3,5},{4,2},{5,3},{6,7},{7,6},{8,9},{9,8},{10,12... | collective-permute-start | bytes 460808 | tf_op jit(solution)/shard_map/ppermute | solution.py:570
  23.4 3.7 %collective-permute-done.2 = f16[600,128]{1,0:T(8,128)(2,1)S(1)} collective-permute-done((f16[600,128]{1,0:T(8,128)(2,1)S(1)}, f16[600,128]{1,0:T(8,128)(2,1)S(1)}, u32[]{:S(2)}, u32[]{:S(2)}) %collective-permute-start.2) | collective-permute-done | bytes 153632 | tf_op jit(solution)/shard_map/ppermute | solution.py:570
  27.2 0.0 collective-permute-done.3
  27.3 1.3 %collective-permute-start.4 = (f16[600,128]{1,0:T(8,128)(2,1)S(1)}, f16[600,128]{1,0:T(8,128)(2,1)S(1)}, u32[]{:S(2)}, u32[]{:S(2)}) collective-permute-start(f16[600,128]{1,0:T(8,128)(2,1)S(1)} %fusion.18), channel_id=1, source_target_pairs={{0,8},{1,9},{2,26},{3,27},{4,28},{5,29},{6,14},{7,15},{8,0},{9,1},... | collective-permute-start | bytes 460808 | tf_op jit(solution)/shard_map/ppermute | solution.py:570
  28.7 5.6 %collective-permute-done.4 = f16[600,128]{1,0:T(8,128)(2,1)S(1)} collective-permute-done((f16[600,128]{1,0:T(8,128)(2,1)S(1)}, f16[600,128]{1,0:T(8,128)(2,1)S(1)}, u32[]{:S(2)}, u32[]{:S(2)}) %collective-permute-start.4) | collective-permute-done | bytes 153632 | tf_op jit(solution)/shard_map/ppermute | solution.py:570
  34.3 0.1 fusion.3
  34.4 3.4 %collective-permute-start.5 = (f16[496,128]{1,0:T(8,128)(2,1)S(1)}, f16[496,128]{1,0:T(8,128)(2,1)S(1)}, u32[]{:S(2)}, u32[]{:S(2)}) collective-permute-start(f16[496,128]{1,0:T(8,128)(2,1)S(1)} %fusion.19), channel_id=1, source_target_pairs={{0,24},{1,25},{2,3},{3,2},{4,5},{5,4},{6,30},{7,31},{8,16},{9,17},... | collective-permute-start | bytes 380936 | tf_op jit(solution)/shard_map/ppermute | solution.py:570
  37.8 0.0 copy-done
  37.8 2.5 %flow.1 = f32[3,16,16,128]{3,2,1,0:T(8,128)} custom-call(f32[3,16,16,128]{3,2,1,0:T(8,128)S(1)} %copy-done, f32[64,128]{1,0:T(8,128)S(1)} %get-tuple-element.27.eddy, f32[104,128]{1,0:T(8,128)S(1)} %slice.81.got0, f32[104,128]{1,0:T(8,128)S(1)} %slice_convert_fusion.2.got1, f32[104,128]{1,0:T(8,128)S(1)} %slice_convert_fusion.1.got2, ...), custom_call_target="tpu_custom_call" | custom-call | tf_op jit(solution)/shard_map/flow/pallas_call | solution.py:439
  40.3 0.9 %collective-permute-done.5 = f16[496,128]{1,0:T(8,128)(2,1)S(1)} collective-permute-done((f16[496,128]{1,0:T(8,128)(2,1)S(1)}, f16[496,128]{1,0:T(8,128)(2,1)S(1)}, u32[]{:S(2)}, u32[]{:S(2)}) %collective-permute-start.5) | collective-permute-done | bytes 127008 | tf_op jit(solution)/shard_map/ppermute | solution.py:570
  41.2 0.0 copy-start.2
  41.3 0.1 collective-permute-start.6
  41.3 1.5 %collective-permute-done.6.other = f32[480,128]{1,0:T(8,128)S(1)} collective-permute-done((f32[480,128]{1,0:T(8,128)S(1)}, f32[480,128]{1,0:T(8,128)S(1)}, u32[]{:S(2)}, u32[]{:S(2)}) %collective-permute-start.6) | collective-permute-done | bytes 245792 | tf_op jit(solution)/shard_map/ppermute | solution.py:587
  42.8 0.0 copy-done.1
  42.8 0.0 copy-done.2
  42.8 1.4 %finish.1 = (f32[1,8]{1,0:T(1,128)}, f32[64,81]{1,0:T(8,128)}, f32[64,1728]{1,0:T(8,128)}, f32[1,64]{1,0:T(1,128)}) custom-call(s32[1,32]{1,0:T(1,128)S(1)} %bitcast.59, s32[1,32]{1,0:T(1,128)S(1)} %bitcast.61, f32[480,128]{1,0:T(8,128)S(1)} %fusion.2.mine, f32[480,128]{1,0:T(8,128)S(1)} %collective-permute-done.6.other), custom_call_target="tpu_custom_call" | custom-call | tf_op jit(solution)/shard_map/finish/pallas_call | solution.py:497
  (26 shorter events, 0.5 us)
Async XLA Ops:
  13.4 1.7 %collective-permute-start = (f32[584,128]{1,0:T(8,128)S(1)}, f32[584,128]{1,0:T(8,128)S(1)}, u32[]{:S(2)}, u32[]{:S(2)}) collective-permute-start(f32[584,128]{1,0:T(8,128)S(1)} %get-tuple-element.21), channel_id=1, source_target_pairs={{0,2},{2,0},{4,6},{6,4},{1,3},{3,1},{5,7},{7,5},{8,10},{10,8},{12,... | collective-permute-start | bytes 897032 | tf_op jit(solution)/shard_map/ppermute | solution.py:549
  15.3 6.4 %collective-permute-start.1 = (f16[600,128]{1,0:T(8,128)(2,1)S(1)}, f16[600,128]{1,0:T(8,128)(2,1)S(1)}, u32[]{:S(2)}, u32[]{:S(2)}) collective-permute-start(f16[600,128]{1,0:T(8,128)(2,1)S(1)} %fusion.14), channel_id=1, source_target_pairs={{0,6},{1,7},{2,10},{3,11},{4,12},{5,13},{6,0},{7,1},{8,14},{9,15},... | collective-permute-start | bytes 460808 | tf_op jit(solution)/shard_map/ppermute | solution.py:570
  18.0 9.2 %collective-permute-start.3 = (f16[104,128]{1,0:T(8,128)(2,1)S(1)}, f16[104,128]{1,0:T(8,128)(2,1)S(1)}, u32[]{:S(2)}, u32[]{:S(2)}) collective-permute-start(f16[104,128]{1,0:T(8,128)(2,1)S(1)} %convert_element_type.91), channel_id=1, source_target_pairs={{0,24},{1,25},{2,3},{3,2},{4,5},{5,4},{6,30},{7,31},{8,16},{9,17},... | collective-permute-start | bytes 79880 | tf_op jit(solution)/shard_map/ppermute | solution.py:565
  21.9 5.3 %collective-permute-start.2 = (f16[600,128]{1,0:T(8,128)(2,1)S(1)}, f16[600,128]{1,0:T(8,128)(2,1)S(1)}, u32[]{:S(2)}, u32[]{:S(2)}) collective-permute-start(f16[600,128]{1,0:T(8,128)(2,1)S(1)} %fusion.16), channel_id=1, source_target_pairs={{0,1},{1,0},{2,4},{3,5},{4,2},{5,3},{6,7},{7,6},{8,9},{9,8},{10,12... | collective-permute-start | bytes 460808 | tf_op jit(solution)/shard_map/ppermute | solution.py:570
  27.3 6.9 %collective-permute-start.4 = (f16[600,128]{1,0:T(8,128)(2,1)S(1)}, f16[600,128]{1,0:T(8,128)(2,1)S(1)}, u32[]{:S(2)}, u32[]{:S(2)}) collective-permute-start(f16[600,128]{1,0:T(8,128)(2,1)S(1)} %fusion.18), channel_id=1, source_target_pairs={{0,8},{1,9},{2,26},{3,27},{4,28},{5,29},{6,14},{7,15},{8,0},{9,1},... | collective-permute-start | bytes 460808 | tf_op jit(solution)/shard_map/ppermute | solution.py:570
  28.7 9.1 %copy-start = (f32[3,16,16,128]{3,2,1,0:T(8,128)S(1)}, f32[3,16,16,128]{3,2,1,0:T(8,128)}, u32[]{:S(2)}) copy-start(f32[3,16,16,128]{3,2,1,0:T(8,128)} %vel.3) | copy-start | bytes 1179652
  34.4 6.8 %collective-permute-start.5 = (f16[496,128]{1,0:T(8,128)(2,1)S(1)}, f16[496,128]{1,0:T(8,128)(2,1)S(1)}, u32[]{:S(2)}, u32[]{:S(2)}) collective-permute-start(f16[496,128]{1,0:T(8,128)(2,1)S(1)} %fusion.19), channel_id=1, source_target_pairs={{0,24},{1,25},{2,3},{3,2},{4,5},{5,4},{6,30},{7,31},{8,16},{9,17},... | collective-permute-start | bytes 380936 | tf_op jit(solution)/shard_map/ppermute | solution.py:570
  41.2 1.6 %copy-start.1 = (s32[1,1,32,1]{2,3,1,0:T(1,128)S(1)}, s32[1,1,32,1]{2,3,1,0:T(1,128)}, u32[]{:S(2)}) copy-start(s32[1,1,32,1]{2,3,1,0:T(1,128)} %param.12) | copy-start | bytes 388
  41.2 1.6 %copy-start.2 = (s32[1,1,32,1]{2,3,1,0:T(1,128)S(1)}, s32[1,1,32,1]{2,3,1,0:T(1,128)}, u32[]{:S(2)}) copy-start(s32[1,1,32,1]{2,3,1,0:T(1,128)} %param.13) | copy-start | bytes 388
  41.3 1.6 %collective-permute-start.6 = (f32[480,128]{1,0:T(8,128)S(1)}, f32[480,128]{1,0:T(8,128)S(1)}, u32[]{:S(2)}, u32[]{:S(2)}) collective-permute-start(f32[480,128]{1,0:T(8,128)S(1)} %fusion.2.mine), channel_id=1, source_target_pairs={{0,2},{2,0},{4,6},{6,4},{1,3},{3,1},{5,7},{7,5},{8,10},{10,8},{12,... | collective-permute-start | bytes 737288 | tf_op jit(solution)/shard_map/ppermute | solution.py:587
